TPU v7x, 256 devices: a whole 4x4x8 slice. The times are simulated.
256 devices in a mesh: section: 16 (over z_lo, y, core), expert: 16 (over x, z_hi).
Axes of the slice: x: 4, y: 4, z: 8 (z_hi: 4, z_lo: 2; z = z_hi * 2 + z_lo), core: 2. Of those that a mesh axis runs over, the one named last changes fastest.
Arguments:
- hidden: bfloat16 [2048, 2048], P(('section', 'expert')), may hold values from -6 to 6
- routes: int32 [2048, 2], P(('section', 'expert')), may hold values from 0 to 15, all different within a row; in each aligned block of 8 rows (0 to 7, 8 to 15, ...) at most 2 rows name the same one
- gates: float32 [2048, 2], P(('section', 'expert')), may hold values from 0.2 to 1
- targets: int32 [2048], replicated, may hold values from 0 to 163839
- target_lengths: int32 [16], replicated, may hold values from 32 to 128
- moe_gain: float32 [2048], replicated, may hold values from 0.5 to 1.5
- fc_in: bfloat16 [16, 2048, 8192], P('expert', None, 'section'), may hold values from -0.125 to 0.125
- fc_out: bfloat16 [16, 8192, 2048], P('expert', 'section'), may hold values from -0.0625 to 0.0625
- final_gain: float32 [2048], replicated, may hold values from 0.5 to 1.5
- head_weight: bfloat16 [2048, 163840], P(None, ('section', 'expert')), may hold values from -6 to 6
Outputs:
- log_probs: bfloat16 [2048, 163840], P(None, ('section', 'expert'))
- head_logits: bfloat16 [2048, 163840], P(None, ('section', 'expert'))
- token_loss: float32 [2048], replicated
Inputs may be any that keep to these rules, and one draw needn't show every extreme that they name: `routes`: within each aligned block of 8 rows (the rows of one device) no expert is named more than 2 times, and the two experts of a row differ.
All inputs are finite; a program needn't handle non-finite values.
Results may differ from a plain program's by a relative error of at most 0.019.
Values may be sent and summed in bfloat16 or wider, within the bound.
A program may use at most 128 MiB of HBM per device.

v0:
```python
import jax
import jax.numpy as jnp
from jax import lax
from jax.sharding import PartitionSpec as P

TGT = 128


def layer_norm(values, scales):
    average = jnp.mean(values, axis=-1, keepdims=True)
    centered = values - average
    spread = jnp.mean(centered * centered, axis=-1, keepdims=True)
    return centered * lax.rsqrt(spread + 1e-05) * scales


def on_device(
    hidden, routes, gates, targets, target_lengths, moe_gain, fc_in, fc_out, final_gain, head_weight
):
    token_rows = hidden.shape[0]
    features = hidden.shape[1]
    groups = lax.axis_size("expert")
    capacity = max(2, (3 * token_rows + groups - 1) // groups)
    residual = hidden.astype(jnp.float32)
    normed = layer_norm(residual, moe_gain).astype(jnp.bfloat16)
    flat_routes = routes.reshape(-1)
    labels = jnp.arange(groups, dtype=jnp.int32)
    matches = (flat_routes[:, None] == labels[None, :]).astype(jnp.int32)
    earlier = jnp.cumsum(matches, axis=0) - matches
    slot_index = jnp.sum(earlier * matches, axis=1)
    placement = flat_routes * capacity + slot_index
    copies = jnp.repeat(normed, 2, axis=0)
    outgoing = jnp.zeros((groups * capacity, features), jnp.bfloat16).at[placement].set(copies)
    outgoing = outgoing.reshape(groups, capacity, features)
    weight_in = fc_in[0]
    weight_out = fc_out[0]
    block_rows = lax.all_gather(
        lax.all_to_all(outgoing, "expert", split_axis=0, concat_axis=0, tiled=True),
        "section",
        axis=0,
        tiled=True,
    )
    sources = block_rows.shape[0]
    slot_count = block_rows.shape[1]
    flattened = block_rows.reshape(sources * slot_count, features)
    hidden_units = jnp.maximum(
        jnp.dot(flattened, weight_in, preferred_element_type=jnp.float32), 0.0
    ).astype(jnp.bfloat16)
    partial_value = jnp.dot(hidden_units, weight_out, preferred_element_type=jnp.float32)
    partials = partial_value.reshape(sources, slot_count, features)
    summed = lax.psum_scatter(
        partials.astype(jnp.bfloat16), "section", scatter_dimension=0, tiled=True
    )
    returned_rows = lax.all_to_all(summed, "expert", split_axis=0, concat_axis=0, tiled=True)
    results = returned_rows.reshape(groups * capacity, features)[placement]
    results = results.astype(jnp.float32).reshape(token_rows, 2, features)
    mixed = residual + gates[:, 0:1] * results[:, 0] + gates[:, 1:2] * results[:, 1]
    final = layer_norm(mixed, final_gain).astype(jnp.bfloat16)
    logits = jnp.dot(
        lax.all_gather(final, ("section", "expert"), axis=0, tiled=True),
        head_weight,
        preferred_element_type=jnp.float32,
    )
    head_logits = logits.astype(jnp.bfloat16)
    vocab_dev = head_weight.shape[1]
    offset = (lax.axis_index("section") * groups + lax.axis_index("expert")) * vocab_dev
    columns = targets - offset
    inside = (columns >= 0) & (columns < vocab_dev)
    clipped = jnp.clip(columns, 0, vocab_dev - 1)
    picked = jnp.where(inside, jnp.take_along_axis(logits, clipped[:, None], axis=1)[:, 0], 0.0)
    local_max = jnp.max(logits, axis=1)
    highest = lax.pmax(local_max, ("section", "expert"))
    local_sum = jnp.sum(jnp.exp(logits - highest[:, None]), axis=1)
    totals, chosen = lax.psum((local_sum, picked), ("section", "expert"))
    log_norm = highest + jnp.log(totals)
    log_probs = (logits - log_norm[:, None]).astype(jnp.bfloat16)
    positions = jnp.arange(targets.shape[0], dtype=jnp.int32)
    lengths = jnp.repeat(target_lengths, TGT)
    token_loss = jnp.where(positions % TGT < lengths, log_norm - chosen, jnp.zeros_like(chosen))
    return (log_probs, head_logits, token_loss)


def solution(mesh):
    return jax.shard_map(
        on_device,
        mesh=mesh,
        in_specs=(
            P(("section", "expert"), None),
            P(("section", "expert"), None),
            P(("section", "expert"), None),
            P(),
            P(),
            P(),
            P("expert", None, "section"),
            P("expert", "section", None),
            P(),
            P(None, ("section", "expert")),
        ),
        out_specs=(P(None, ("section", "expert")), P(None, ("section", "expert")), P()),
        check_vma=False,
    )
```

profile of v0, /device:TPU:1, one launch (start us, length us, event | category | flops | bytes accessed | tf_op | source)
XLA Modules:
  0.0 1161.0 jit_solution(9577197982127611084)
XLA Ops:
  7.2 0.9 copy.29
  9.4 0.9 convert_reduce_fusion
  10.3 1.0 fusion.12
  11.2 0.8 fusion.14
  12.2 0.7 scatter_custom_fusion
  13.0 21.0 %all_to_all.10 = bf16[16,2,2048]{2,1,0:T(2,128)(2,1)} all-to-all(bf16[16,2,2048]{2,1,0:T(2,128)(2,1)S(1)} %reshape.108), channel_id=1, replica_groups=mesh['section'=16,'expert'=16] {'expert'}, dimensions={0} | all-to-all | bytes 262144 | tf_op jit(solution)/shard_map/all_to_all | solution.py:37
  34.1 33.5 %all-gather.3.cloned.1.call-done = bf16[256,2,2048]{2,1,0:T(2,128)(2,1)} async-done(((bf16[16,2,2048]{2,1,0:T(2,128)(2,1)}), bf16[256,2,2048]{2,1,0:T(2,128)(2,1)}) %all-gather.3.cloned.1.call-update) | async-done | bytes 2097168 | tf_op jit(solution)/shard_map/all_gather | solution.py:36
  67.6 4.1 reshape.109
  71.7 3.5 fusion.6
  75.2 1.0 dot_general.12
  76.2 4.3 convolution_convert_fusion
  80.6 62.2 %reduce-scatter.2.cloned.1.call-done = bf16[16,2,2048]{2,0,1:T(8,128)(2,1)} async-done(((bf16[256,2,2048]{2,0,1:T(8,128)(2,1)}), bf16[16,2,2048]{2,0,1:T(8,128)(2,1)}) %reduce-scatter.2.cloned.1.call-update) | async-done | bytes 131088 | tf_op jit(solution)/shard_map/reduce_scatter | solution.py:50
  142.8 1.7 copy.31
  144.5 9.0 all-to-all-start.1
  153.6 9.4 all-to-all-done.1
  165.1 714.8 %all-gather.5.cloned.1.call-done = bf16[2048,2048]{1,0:T(8,128)(2,1)} async-done(((bf16[8,2048]{1,0:T(8,128)(2,1)}), bf16[2048,2048]{1,0:T(8,128)(2,1)}) %all-gather.5.cloned.1.call-update) | async-done | bytes 8388624 | tf_op jit(solution)/shard_map/all_gather | solution.py:59
  880.0 9.6 fusion.33
  889.5 78.7 %pmax.7 = f32[2048]{0:T(1024)S(1)} all-reduce(f32[2048]{0:T(1024)S(1)} %get-tuple-element.24), channel_id=1, replica_groups=mesh['section'=16,'expert'=16] {'section','expert'}, use_global_device_ids=true, to_apply=%region_9.10 | all-reduce | flops 2048 | bytes 16384 | tf_op jit(solution)/shard_map/pmax | solution.py:71
  968.2 3.2 exponential_reduce_fusion
  971.4 89.8 %gather_fusion.1 = f32[2048]{0:T(1024)S(1)} fusion(f32[2048,640]{0,1:T(8,128)} %get-tuple-element.25, s32[2048]{0:T(1024)S(1)} %bitcast.46), kind=kCustom, calls=%fused_computation.1 | custom fusion | bytes 32768 | tf_op jit(solution)/shard_map/jit(take_along_axis)/gather | solution.py:69
  1061.2 76.3 %all-reduce = (f32[2048]{0:T(1024)S(1)}, f32[2048]{0:T(1024)S(1)}) all-reduce(f32[2048]{0:T(1024)S(1)} %exponential_reduce_fusion, f32[2048]{0:T(1024)S(1)} %select_select_fusion), channel_id=1, replica_groups=mesh['section'=16,'expert'=16] {'section','expert'}, use_global_device_ids=true, to_apply=%region_11.12 | all-reduce | flops 4096 | bytes 32768 | tf_op jit(solution)/shard_map/psum | solution.py:73
  1138.2 7.5 fusion.31
  1145.7 4.4 copy.34
  1150.1 4.4 copy.35
  (48 shorter events, 4.3 us)
Async XLA Ops:
  7.2 872.8 %copy-start = (bf16[2048,640]{1,0:T(8,128)(2,1)S(1)}, bf16[2048,640]{1,0:T(8,128)(2,1)}, u32[]{:S(2)}) copy-start(bf16[2048,640]{1,0:T(8,128)(2,1)} %param.19) | copy-start | bytes 7864324
  7.2 60.5 %all-gather.3.cloned.1.call-start = ((), (), s32[]{:S(2)}) async-start(), calls=%async_computation.3 | async-start | bytes 2228224 | tf_op jit(solution)/shard_map/all_gather | solution.py:36
  34.1 108.7 %reduce-scatter.2.cloned.1.call-start = ((), (), s32[]{:S(2)}) async-start(), calls=%async_computation.4 | async-start | bytes 2228224 | tf_op jit(solution)/shard_map/reduce_scatter | solution.py:50
  80.6 73.0 %copy-start.4 = (f32[8,2]{0,1:T(2,128)S(1)}, f32[8,2]{0,1:T(2,128)}, u32[]{:S(2)}) copy-start(f32[8,2]{0,1:T(2,128)} %param.12) | copy-start | bytes 196
  80.6 83.3 %copy-start.1 = (bf16[8,2048]{1,0:T(8,128)(2,1)S(1)}, bf16[8,2048]{1,0:T(8,128)(2,1)}, u32[]{:S(2)}) copy-start(bf16[8,2048]{1,0:T(8,128)(2,1)} %param.10) | copy-start | bytes 98308
  80.6 83.7 %copy-start.3 = (f32[2048]{0:T(1024)S(1)}, f32[2048]{0:T(1024)}, u32[]{:S(2)}) copy-start(f32[2048]{0:T(1024)} %param.18) | copy-start | bytes 24580
  80.6 84.5 %copy-start.2 = (s32[2048]{0:T(1024)S(1)}, s32[2048]{0:T(1024)}, u32[]{:S(2)}) copy-start(s32[2048]{0:T(1024)} %param.13) | copy-start | bytes 24580
  144.5 18.5 %all-to-all-start.1 = ((bf16[16,2,2048]{2,1,0:T(2,128)(2,1)}), bf16[16,2,2048]{2,1,0:T(2,128)(2,1)S(1)}, u32[]{:S(2)}, u32[]{:S(2)}) async-start(bf16[16,2,2048]{2,1,0:T(2,128)(2,1)} %copy.31), calls=%async_computation.2 | async-start | bytes 262144 | tf_op jit(solution)/shard_map/all_to_all | solution.py:53
  153.5 726.5 %all-gather.5.cloned.1.call-start = ((), (), s32[]{:S(2)}) async-start(), calls=%async_computation.5 | async-start | bytes 8421376 | tf_op jit(solution)/shard_map/all_gather | solution.py:59
  971.4 166.1 %copy-start.5 = (s32[16]{0:T(128)S(1)}, s32[16]{0:T(128)}, u32[]{:S(2)}) copy-start(s32[16]{0:T(128)} %param.14) | copy-start | bytes 196
Sparse Core Ops, SparseCore 0:
  34.2 33.4 all-gather.2
  80.7 62.0 reduce-scatter.1
  165.1 714.7 all-gather.4
where the time goes:
time: 1160 us
  waiting for transfers between devices  820 us (71%)
  blocking collectives  176 us (15%)
  local copies, waits for them, and re-layouts  108 us (9%)
  matrix products  17.4 us (1%)
  other arithmetic  16.3 us (1%)
  between operations  13.9 us (1%)
    all_gather x1, waiting for transfers between devices, on_device(): lax.all_gather(final, ('section', 'expert'), axis=0, tiled=True)  715 us
    gather x1, local copies, waits for them, and re-layouts, on_device(): jnp.take_along_axis(logits, clipped[:, None], axis=1)[:, 0]  89.8 us
    pmax x1, blocking collectives, on_device(): highest = lax.pmax(local_max, ('section', 'expert'))  78.7 us
    psum x1, blocking collectives, on_device(): totals, chosen = lax.psum((local_sum, picked), ('section', 'expert'))  76.3 us
    reduce_scatter x1, waiting for transfers between devices, on_device(): lax.psum_scatter(partials.astype(jnp.bfloat16), 'section', scatter_dimens...  62.2 us
    all_gather x1, waiting for transfers between devices, on_device(): lax.all_gather(lax.all_to_all(outgoing, 'expert', split_axis=0, concat_ax...  33.5 us
  transfers between devices with their start and end apart: 4, of which 4 were waited for; matrix products, arithmetic and copies ran while one was open for 0% of the time, Pallas kernels for 0%

commit v1 on v0

--- a/solution.py
+++ b/solution.py
@@ -1,9 +1,14 @@
 import jax
 import jax.numpy as jnp
 from jax import lax
+from jax.experimental import pallas as pl
+from jax.experimental.pallas import tpu as pltpu
 from jax.sharding import PartitionSpec as P
 
 TGT = 128
+MESH = pl.DeviceIdType.MESH
+HALF = 1024
+PIECES = 8
 
 
 def layer_norm(values, scales):
@@ -11,6 +16,306 @@
     centered = values - average
     spread = jnp.mean(centered * centered, axis=-1, keepdims=True)
     return centered * lax.rsqrt(spread + 1e-05) * scales
+
+
+class Place:
+    def __init__(self):
+        self.s = lax.axis_index("section")
+        self.e = lax.axis_index("expert")
+        self.core = lax.rem(self.s, 2)
+        self.y = lax.rem(lax.div(self.s, 2), 4)
+        self.zl = lax.div(self.s, 8)
+        self.x = lax.div(self.e, 4)
+        self.zh = lax.rem(self.e, 4)
+        self.z = self.zh * 2 + self.zl
+        self.sibling = (self.s + 1 - 2 * self.core, self.e)
+
+    def at(self, axis):
+        return {"x": self.x, "y": self.y, "z": self.z}[axis]
+
+    def beside(self, axis, step):
+        x, y, z = self.x, self.y, self.z
+        if axis == "x":
+            x = lax.rem(x + step + 4, 4)
+        elif axis == "y":
+            y = lax.rem(y + step + 4, 4)
+        else:
+            z = lax.rem(z + step + 8, 8)
+        return ((lax.rem(z, 2) * 4 + y) * 2 + self.core, x * 4 + lax.div(z, 2))
+
+
+def remote(src, dst, send, recv, to):
+    return pltpu.make_async_remote_copy(
+        src_ref=src, dst_ref=dst, send_sem=send, recv_sem=recv, device_id=to, device_id_type=MESH
+    )
+
+
+ORDERS = ((("x", 4), ("y", 4), ("z", 8)), (("z", 8), ("x", 4), ("y", 4)))
+
+
+def view(g, core, phase, where, pos, part):
+    lanes = slice(None) if part is None else pl.ds(part * (HALF // 2), HALF // 2)
+    if core == 0:
+        if phase == 0:
+            return g.at[0, where.zl, where.y, pos, where.zh, :, lanes]
+        if phase == 1:
+            return g.at[0, where.zl, pos, :, where.zh, :, lanes]
+        return g.at[0, lax.rem(pos, 2), :, :, lax.div(pos, 2), :, lanes]
+    if phase == 0:
+        return g.at[1, lax.rem(pos, 2), where.y, where.x, lax.div(pos, 2), :, lanes]
+    if phase == 1:
+        return g.at[1, :, where.y, pos, :, :, lanes]
+    return g.at[1, :, pos, :, :, :, lanes]
+
+
+def arrivals(g, core, where):
+    for phase, (axis, n) in enumerate(ORDERS[core]):
+        me = where.at(axis)
+        for step in range(1, n // 2 + 1):
+            last = step == n // 2
+            parts = (0, 1) if last else (None, None)
+            sends = (
+                view(g, core, phase, where, lax.rem(me - step + 1 + n, n), parts[0]),
+                view(g, core, phase, where, lax.rem(me + step - 1, n), parts[1]),
+            )
+            lands = (
+                view(g, core, phase, where, lax.rem(me - step + n, n), parts[0]),
+                view(g, core, phase, where, lax.rem(me + step, n), parts[1]),
+            )
+            yield axis, sends, lands
+
+
+def gather(core, where, g, ring_send, ring_recv, pair_send, pair_recv):
+    own = g.at[core, where.zl, where.y, where.x, where.zh]
+    shared = [(own, remote(own, own, pair_send.at[0], pair_recv.at[0], where.sibling))]
+    shared[0][1].start()
+    sent = []
+    k = 0
+    for axis, sends, lands in arrivals(g, core, where):
+        for side in (0, 1):
+            to = where.beside(axis, 1 - 2 * side)
+            copy = remote(sends[side], sends[side], ring_send.at[k + side], ring_recv.at[k + side], to)
+            copy.start()
+            sent.append(copy)
+        for side in (0, 1):
+            landed = lands[side]
+            remote(
+                landed, landed, ring_send.at[k + side], ring_recv.at[k + side], where.beside(axis, 2 * side - 1)
+            ).wait_recv()
+            copy = remote(landed, landed, pair_send.at[1 + k + side], pair_recv.at[1 + k + side], where.sibling)
+            copy.start()
+            shared.append((landed, copy))
+        k += 2
+    other = g.at[1 - core, where.zl, where.y, where.x, where.zh]
+    remote(other, other, pair_send.at[0], pair_recv.at[0], where.sibling).wait_recv()
+    k = 1
+    for _, _, lands in arrivals(g, 1 - core, where):
+        for side in (0, 1):
+            landed = lands[side]
+            remote(landed, landed, pair_send.at[k], pair_recv.at[k], where.sibling).wait_recv()
+            k += 1
+    for copy in sent:
+        copy.wait_send()
+    for _, copy in shared:
+        copy.wait_send()
+
+
+def exchange(n, me, to, src, dst, send, recv):
+    def each(i, _):
+        other = lax.rem(me + i, n)
+        remote(src(other), dst.at[me], send.at[i], recv.at[i], to(other)).start()
+        return 0
+
+    lax.fori_loop(1, n, each, 0)
+
+    def done(i, _):
+        origin = lax.rem(me - i + n, n)
+        copy = remote(src(origin), dst.at[origin], send.at[i], recv.at[i], to(origin))
+        copy.wait_recv()
+        copy.wait_send()
+        return 0
+
+    lax.fori_loop(1, n, done, 0)
+
+
+def merge(stats):
+    high = stats[:, 0:1, :]
+    top = jnp.max(high, axis=0)
+    total = jnp.sum(stats[:, 1:2, :] * jnp.exp(high - top[None]), axis=0)
+    return top, total, jnp.sum(stats[:, 2:3, :], axis=0)
+
+
+def rows8(first, second, third):
+    row = lax.broadcasted_iota(jnp.int32, (8, 128), 0)
+    zero = jnp.zeros((8, 128), jnp.float32)
+    out = jnp.where(row == 0, first, zero)
+    out = jnp.where(row == 1, second, out)
+    return jnp.where(row == 2, third, out)
+
+
+def head_kernel(
+    final_ref, targets_ref, weight_hbm, logits_hbm, norms_ref,
+    g, weight, logits, halves, stats, by_group, by_section, merged, solved,
+    weight_sem, out_sem, swap_send, swap_recv, ring_send, ring_recv, pair_send, pair_recv,
+    one_send, one_recv, two_send, two_recv, three_send, three_recv,
+):
+    where = Place()
+    barrier = pltpu.get_barrier_semaphore()
+    load = pltpu.make_async_copy(weight_hbm, weight, weight_sem)
+    load.start()
+
+    def greet(i, _):
+        pl.semaphore_signal(
+            barrier, inc=1, device_id=(lax.rem(where.s + i, 16), where.e), device_id_type=MESH
+        )
+        pl.semaphore_signal(
+            barrier, inc=1, device_id=(where.s, lax.rem(where.e + i, 16)), device_id_type=MESH
+        )
+        return 0
+
+    lax.fori_loop(1, 16, greet, 0)
+    for step in (1, -1):
+        pl.semaphore_signal(barrier, inc=1, device_id=where.beside("z", step), device_id_type=MESH)
+    pl.semaphore_wait(barrier, 32)
+
+    for core in (0, 1):
+
+        @pl.when(where.core == core)
+        def _():
+            away = final_ref.at[:, pl.ds((1 - core) * HALF, HALF)]
+            swap = remote(away, halves, swap_send, swap_recv, where.sibling)
+            swap.start()
+            swap.wait()
+            mine = final_ref[:, core * HALF : (core + 1) * HALF]
+            both = (mine, halves[...]) if core == 0 else (halves[...], mine)
+            g[core, where.zl, where.y, where.x, where.zh] = jnp.concatenate(both, axis=0).astype(jnp.bfloat16)
+            gather(core, where, g, ring_send, ring_recv, pair_send, pair_recv)
+
+    load.wait()
+    columns = weight.shape[1]
+    offset = (where.s * 16 + where.e) * columns
+    lane = lax.broadcasted_iota(jnp.int32, (128, 128), 1)
+
+    def chunk(i, _):
+        zl, y = lax.div(i, 4), lax.rem(i, 4)
+        low = g[0, zl, y].reshape(256, HALF)
+        high = g[1, zl, y].reshape(256, HALF)
+        found = jnp.dot(low, weight[0:HALF], preferred_element_type=jnp.float32)
+        found = found + jnp.dot(high, weight[HALF:], preferred_element_type=jnp.float32)
+        found = found.reshape(16, 2, 8, columns)
+        for core in (0, 1):
+            group = i * 2 + core
+            part = found[:, core].reshape(128, columns)
+            logits[pl.ds(group * 128, 128), :] = part
+            top = jnp.max(part, axis=1, keepdims=True)
+            total = jnp.sum(jnp.exp(part - top), axis=1, keepdims=True)
+            wanted = jnp.transpose(jnp.broadcast_to(targets_ref[pl.ds(group, 1), :], (128, 128)))
+            picked = jnp.zeros((128, 128), jnp.float32)
+            for tile in range(columns // 128):
+                ids = (lane + (offset + tile * 128)).astype(jnp.float32)
+                picked = picked + jnp.where(ids == wanted, part[:, tile * 128 : (tile + 1) * 128], 0.0)
+            picked = jnp.sum(picked, axis=1, keepdims=True)
+            table = jnp.where(lane == 0, top, jnp.where(lane == 1, total, jnp.where(lane == 2, picked, 0.0)))
+            stats[group] = jnp.transpose(table)[0:8]
+        pltpu.make_async_copy(
+            logits.at[pl.ds(i * 256, 256)], logits_hbm.at[pl.ds(i * 256, 256)], out_sem.at[i]
+        ).start()
+        return 0
+
+    lax.fori_loop(0, PIECES, chunk, 0)
+
+    to_expert = lambda other: (where.s, other)
+    to_section = lambda other: (other, where.e)
+    by_group[where.e] = stats[where.e]
+    exchange(16, where.e, to_expert, lambda other: stats.at[other], by_group, one_send, one_recv)
+    merged[...] = rows8(*merge(by_group[...]))
+    by_section[where.s] = merged[...]
+    exchange(16, where.s, to_section, lambda other: merged, by_section, two_send, two_recv)
+    top, total, picked = merge(by_section[...])
+    log_norm = top + jnp.log(total)
+    solved[...] = rows8(log_norm, log_norm - picked, jnp.zeros_like(picked))
+    norms_ref[where.e] = solved[...]
+    exchange(16, where.e, to_expert, lambda other: solved, norms_ref, three_send, three_recv)
+
+    def stored(i, _):
+        pltpu.make_async_copy(
+            logits.at[pl.ds(i * 256, 256)], logits_hbm.at[pl.ds(i * 256, 256)], out_sem.at[i]
+        ).wait()
+        return 0
+
+    lax.fori_loop(0, PIECES, stored, 0)
+
+
+def head(final, targets, weight):
+    features, columns = weight.shape
+    tokens = targets.size
+    dma = pltpu.SemaphoreType.DMA
+    return pl.pallas_call(
+        head_kernel,
+        name="head",
+        out_shape=(
+            jax.ShapeDtypeStruct((tokens, columns), jnp.float32),
+            jax.ShapeDtypeStruct((16, 8, 128), jnp.float32),
+        ),
+        in_specs=[
+            pl.BlockSpec(memory_space=pltpu.VMEM),
+            pl.BlockSpec(memory_space=pltpu.VMEM),
+            pl.BlockSpec(memory_space=pl.ANY),
+        ],
+        out_specs=(pl.BlockSpec(memory_space=pl.ANY), pl.BlockSpec(memory_space=pltpu.VMEM)),
+        scratch_shapes=[
+            pltpu.VMEM((2, 2, 4, 4, 4, 16, HALF), jnp.bfloat16),
+            pltpu.VMEM((features, columns), jnp.bfloat16),
+            pltpu.VMEM((tokens, columns), jnp.float32),
+            pltpu.VMEM((8, HALF), jnp.float32),
+            pltpu.VMEM((16, 8, 128), jnp.float32),
+            pltpu.VMEM((16, 8, 128), jnp.float32),
+            pltpu.VMEM((16, 8, 128), jnp.float32),
+            pltpu.VMEM((8, 128), jnp.float32),
+            pltpu.VMEM((8, 128), jnp.float32),
+            dma, dma((PIECES,)), dma, dma,
+            dma((16,)), dma((16,)), dma((17,)), dma((17,)),
+            dma((16,)), dma((16,)), dma((16,)), dma((16,)), dma((16,)), dma((16,)),
+        ],
+        compiler_params=pltpu.CompilerParams(
+            collective_id=1, has_side_effects=True, vmem_limit_bytes=48 * 1024 * 1024
+        ),
+    )(final, targets, weight)
+
+
+def finish_kernel(logits_ref, norms_ref, lengths_ref, probs_ref, head_ref, loss_ref):
+    values = logits_ref[...]
+    head_ref[...] = values.astype(jnp.bfloat16)
+    shift = jnp.transpose(jnp.broadcast_to(norms_ref[0, 0:1, :], (128, 128)))
+    for tile in range(values.shape[1] // 128):
+        lanes = slice(tile * 128, (tile + 1) * 128)
+        probs_ref[:, lanes] = (values[:, lanes] - shift).astype(jnp.bfloat16)
+
+    position = lax.broadcasted_iota(jnp.int32, (1, 128), 1)
+    group = pl.program_id(0)
+    loss_ref[pl.ds(group, 1), :] = jnp.where(position < lengths_ref[group], norms_ref[0, 1:2, :], 0.0)
+
+
+def finish(logits, norms, lengths):
+    tokens, columns = logits.shape
+    groups = tokens // TGT
+    rows = pl.BlockSpec((TGT, columns), lambda i: (i, 0))
+    return pl.pallas_call(
+        finish_kernel,
+        name="finish",
+        grid=(groups,),
+        out_shape=(
+            jax.ShapeDtypeStruct((tokens, columns), jnp.bfloat16),
+            jax.ShapeDtypeStruct((tokens, columns), jnp.bfloat16),
+            jax.ShapeDtypeStruct((groups, TGT), jnp.float32),
+        ),
+        in_specs=[
+            rows,
+            pl.BlockSpec((1, 8, 128), lambda i: (i, 0, 0)),
+            pl.BlockSpec(memory_space=pltpu.SMEM),
+        ],
+        out_specs=(rows, rows, pl.BlockSpec((groups, TGT), lambda i: (0, 0))),
+    )(logits, norms, lengths)
 
 
 def on_device(
@@ -55,28 +360,10 @@
     results = results.astype(jnp.float32).reshape(token_rows, 2, features)
     mixed = residual + gates[:, 0:1] * results[:, 0] + gates[:, 1:2] * results[:, 1]
     final = layer_norm(mixed, final_gain).astype(jnp.bfloat16)
-    logits = jnp.dot(
-        lax.all_gather(final, ("section", "expert"), axis=0, tiled=True),
-        head_weight,
-        preferred_element_type=jnp.float32,
-    )
-    head_logits = logits.astype(jnp.bfloat16)
-    vocab_dev = head_weight.shape[1]
-    offset = (lax.axis_index("section") * groups + lax.axis_index("expert")) * vocab_dev
-    columns = targets - offset
-    inside = (columns >= 0) & (columns < vocab_dev)
-    clipped = jnp.clip(columns, 0, vocab_dev - 1)
-    picked = jnp.where(inside, jnp.take_along_axis(logits, clipped[:, None], axis=1)[:, 0], 0.0)
-    local_max = jnp.max(logits, axis=1)
-    highest = lax.pmax(local_max, ("section", "expert"))
-    local_sum = jnp.sum(jnp.exp(logits - highest[:, None]), axis=1)
-    totals, chosen = lax.psum((local_sum, picked), ("section", "expert"))
-    log_norm = highest + jnp.log(totals)
-    log_probs = (logits - log_norm[:, None]).astype(jnp.bfloat16)
-    positions = jnp.arange(targets.shape[0], dtype=jnp.int32)
-    lengths = jnp.repeat(target_lengths, TGT)
-    token_loss = jnp.where(positions % TGT < lengths, log_norm - chosen, jnp.zeros_like(chosen))
-    return (log_probs, head_logits, token_loss)
+    wanted = targets.astype(jnp.float32).reshape(-1, TGT)
+    logits, norms = head(final.astype(jnp.float32), wanted, head_weight)
+    log_probs, head_logits, loss = finish(logits, norms, target_lengths)
+    return (log_probs, head_logits, loss.reshape(-1))
 
 
 def solution(mesh):

time: 1160 us -> 267 us (0.23)
  waiting for transfers between devices: 820 us -> 105 us
  blocking collectives: 176 us -> 21 us
  local copies, waits for them, and re-layouts: 108 us -> 11.8 us
  Pallas kernels: 0 us -> 94.9 us
  other arithmetic: 16.3 us -> 4.34 us
    all_gather x1 -> x0, waiting for transfers between devices: 715 us -> none  [on_device(): lax.all_gather(final, ('section', 'expert'), axis=0, tiled=True)]
    pallas_call x0 -> x2, Pallas kernels: none -> 94.9 us  [the longest x1 84.1 us: head(): pl.pallas_call(head_kernel, name='head', out_shape=(jax.ShapeDtypeStruct(...]
    gather x1 -> x0, local copies, waits for them, and re-layouts: 89.8 us -> none  [on_device(): jnp.take_along_axis(logits, clipped[:, None], axis=1)[:, 0]]
    pmax x1 -> x0, blocking collectives: 78.7 us -> none  [on_device(): highest = lax.pmax(local_max, ('section', 'expert'))]
    psum x1 -> x0, blocking collectives: 76.3 us -> none  [on_device(): totals, chosen = lax.psum((local_sum, picked), ('section', 'expert'))]
  transfers between devices with their start and end apart: 4 -> 3, of which waited for: 4 -> 3; matrix products, arithmetic and copies ran while one was open for 0% -> 0% of each run, Pallas kernels for 0% -> 0%
where the time goes in v1:
time: 267 us; the launch traced here: 266 us
  waiting for transfers between devices  105 us (39%)
  Pallas kernels  94.9 us (36%)
  blocking collectives  21 us (8%)
  between operations  14.2 us (5%)
  local copies, waits for them, and re-layouts  11.8 us (4%)
  starting transfers between devices  9.06 us (3%)
  matrix products  6.05 us (2%)
  other arithmetic  4.34 us (2%)
    pallas_call x1, Pallas kernels, head(): pl.pallas_call(head_kernel, name='head', out_shape=(jax.ShapeDtypeStruct(...  84.1 us
    reduce_scatter x1, waiting for transfers between devices, on_device(): lax.psum_scatter(partials.astype(jnp.bfloat16), 'section', scatter_dimens...  61.6 us
    all_gather x1, waiting for transfers between devices, on_device(): lax.all_gather(lax.all_to_all(outgoing, 'expert', split_axis=0, concat_ax...  33.5 us
    all_to_all x1, blocking collectives, on_device(): lax.all_to_all(outgoing, 'expert', split_axis=0, concat_axis=0, tiled=True)  21 us
    pallas_call x1, Pallas kernels, finish(): pl.pallas_call(finish_kernel, name='finish', grid=(groups,), out_shape=(j...  10.7 us
    all_to_all x1, waiting for transfers between devices, on_device(): lax.all_to_all(summed, 'expert', split_axis=0, concat_axis=0, tiled=True)  9.47 us
    all_to_all x1, starting transfers between devices, on_device(): lax.all_to_all(summed, 'expert', split_axis=0, concat_axis=0, tiled=True)  8.98 us
  transfers between devices with their start and end apart: 3, of which 3 were waited for; matrix products, arithmetic and copies ran while one was open for 0% of the time, Pallas kernels for 0%

profile of v1, /device:TPU:1, one launch (start us, length us, event | category | flops | bytes accessed | tf_op | source)
XLA Modules:
  0.0 265.9 jit_solution(13491305968773978336)
XLA Ops:
  7.2 0.8 broadcast_multiply_fusion
  8.0 0.8 copy.23
  8.8 0.9 convert_reduce_fusion
  9.7 1.0 fusion.12
  11.2 0.8 fusion.14
  12.2 0.7 scatter_custom_fusion
  13.0 21.0 %all_to_all.10 = bf16[16,2,2048]{2,1,0:T(2,128)(2,1)} all-to-all(bf16[16,2,2048]{2,1,0:T(2,128)(2,1)S(1)} %reshape.87), channel_id=1, replica_groups=mesh['section'=16,'expert'=16] {'expert'}, dimensions={0} | all-to-all | bytes 262144 | tf_op jit(solution)/shard_map/all_to_all | solution.py:342
  34.1 33.5 %all-gather.2.cloned.1.call-done = bf16[256,2,2048]{2,1,0:T(2,128)(2,1)} async-done(((bf16[16,2,2048]{2,1,0:T(2,128)(2,1)}), bf16[256,2,2048]{2,1,0:T(2,128)(2,1)}) %all-gather.2.cloned.1.call-update) | async-done | bytes 2097168 | tf_op jit(solution)/shard_map/all_gather | solution.py:341
  67.6 4.1 %reshape.88 = bf16[512,2048]{1,0:T(8,128)(2,1)} reshape(bf16[256,2,2048]{2,1,0:T(2,128)(2,1)} %all-gather.2.cloned.1.call-done) | data formatting | bytes 4194304 | tf_op jit(solution)/shard_map/reshape | solution.py:349
  71.7 3.5 %fusion.6 = bf16[512,512]{1,0:T(8,128)(2,1)S(1)} fusion(bf16[512,2048]{1,0:T(8,128)(2,1)} %reshape.88, bf16[1,2048,512]{2,1,0:T(8,128)(2,1)} %param.16), kind=kOutput, calls=%fused_computation.7 | convolution fusion | flops 1074266112 | bytes 4718592 | tf_op jit(solution)/shard_map/dot_general | solution.py:351
  75.2 0.2 dot_general.9
  75.4 2.6 convolution_convert_fusion
  78.0 0.6 copy-done.6
  78.7 61.6 %reduce-scatter.2.cloned.1.call-done = bf16[16,2,2048]{2,0,1:T(8,128)(2,1)} async-done(((bf16[256,2,2048]{2,0,1:T(8,128)(2,1)}), bf16[16,2,2048]{2,0,1:T(8,128)(2,1)}) %reduce-scatter.2.cloned.1.call-update) | async-done | bytes 131088 | tf_op jit(solution)/shard_map/reduce_scatter | solution.py:355
  140.3 1.7 copy.25
  142.0 9.0 %all-to-all-start.1 = ((bf16[16,2,2048]{2,1,0:T(2,128)(2,1)}), bf16[16,2,2048]{2,1,0:T(2,128)(2,1)S(1)}, u32[]{:S(2)}, u32[]{:S(2)}) async-start(bf16[16,2,2048]{2,1,0:T(2,128)(2,1)} %copy.25), calls=%async_computation.2 | async-start | bytes 262144 | tf_op jit(solution)/shard_map/all_to_all | solution.py:358
  151.0 9.5 %all-to-all-done.1 = bf16[16,2,2048]{2,1,0:T(2,128)(2,1)S(1)} async-done(((bf16[16,2,2048]{2,1,0:T(2,128)(2,1)}), bf16[16,2,2048]{2,1,0:T(2,128)(2,1)S(1)}, u32[]{:S(2)}, u32[]{:S(2)}) %all-to-all-start.1) | async-done | bytes 131104 | tf_op jit(solution)/shard_map/all_to_all | solution.py:358
  160.5 0.6 gather_fusion
  161.3 0.2 fusion.23
  161.5 0.2 multiply_reduce_fusion
  161.8 1.7 copy-done.1
  163.6 84.1 %head.1 = (f32[2048,640]{1,0:T(8,128)}, f32[16,8,128]{2,1,0:T(8,128)S(1)}) custom-call(f32[8,2048]{1,0:T(8,128)S(1)} %fusion.20.final_ref, f32[16,128]{1,0:T(8,128)S(1)} %convert_bitcast_fusion.targets_ref, bf16[2048,640]{1,0:T(8,128)(2,1)S(1)} %copy-done.1), custom_call_target="tpu_custom_call" | custom-call | tf_op jit(solution)/shard_map/head/pallas_call | solution.py:253
  247.7 0.6 copy-done.2
  248.3 10.7 %finish.1 = (bf16[2048,640]{1,0:T(8,128)(2,1)}, bf16[2048,640]{1,0:T(8,128)(2,1)}, f32[16,128]{1,0:T(8,128)}) custom-call(f32[2048,640]{1,0:T(8,128)} %get-tuple-element.8.logits_ref, f32[16,8,128]{2,1,0:T(8,128)} %copy-done.2, s32[16]{0:T(128)} %lengths_ref.1), custom_call_target="tpu_custom_call" | custom-call | tf_op jit(solution)/shard_map/finish/pallas_call | solution.py:303
  (36 shorter events, 1.2 us)
Async XLA Ops:
  7.2 68.2 %copy-start = (bf16[1,512,2048]{2,1,0:T(8,128)(2,1)S(1)}, bf16[1,512,2048]{2,1,0:T(8,128)(2,1)}, u32[]{:S(2)}) copy-start(bf16[1,512,2048]{2,1,0:T(8,128)(2,1)} %param.17) | copy-start | bytes 6291460
  7.2 60.4 %all-gather.2.cloned.1.call-start = ((), (), s32[]{:S(2)}) async-start(), calls=%async_computation.3 | async-start | bytes 2228224 | tf_op jit(solution)/shard_map/all_gather | solution.py:341
  34.1 106.2 %reduce-scatter.2.cloned.1.call-start = ((), (), s32[]{:S(2)}) async-start(), calls=%async_computation.4 | async-start | bytes 2228224 | tf_op jit(solution)/shard_map/reduce_scatter | solution.py:355
  78.0 0.7 copy-start.6
  78.0 73.0 %copy-start.5 = (s32[2048]{0:T(1024)S(1)}, s32[2048]{0:T(1024)}, u32[]{:S(2)}) copy-start(s32[2048]{0:T(1024)} %param.13) | copy-start | bytes 24580
  78.0 83.3 %copy-start.3 = (bf16[8,2048]{1,0:T(8,128)(2,1)S(1)}, bf16[8,2048]{1,0:T(8,128)(2,1)}, u32[]{:S(2)}) copy-start(bf16[8,2048]{1,0:T(8,128)(2,1)} %param.10) | copy-start | bytes 98308
  78.0 83.7 %copy-start.4 = (f32[2048]{0:T(1024)S(1)}, f32[2048]{0:T(1024)}, u32[]{:S(2)}) copy-start(f32[2048]{0:T(1024)} %param.18) | copy-start | bytes 24580
  142.0 18.5 %all-to-all-start.1 = ((bf16[16,2,2048]{2,1,0:T(2,128)(2,1)}), bf16[16,2,2048]{2,1,0:T(2,128)(2,1)S(1)}, u32[]{:S(2)}, u32[]{:S(2)}) async-start(bf16[16,2,2048]{2,1,0:T(2,128)(2,1)} %copy.25), calls=%async_computation.2 | async-start | bytes 262144 | tf_op jit(solution)/shard_map/all_to_all | solution.py:358
  161.8 1.7 copy-start.1
  247.7 0.6 copy-start.2
Sparse Core Ops, SparseCore 0:
  34.2 33.4 all-gather.1
  78.2 62.0 reduce-scatter.1

commit v2 on v1

--- a/solution.py
+++ b/solution.py
@@ -9,13 +9,7 @@
 MESH = pl.DeviceIdType.MESH
 HALF = 1024
 PIECES = 8
-
-
-def layer_norm(values, scales):
-    average = jnp.mean(values, axis=-1, keepdims=True)
-    centered = values - average
-    spread = jnp.mean(centered * centered, axis=-1, keepdims=True)
-    return centered * lax.rsqrt(spread + 1e-05) * scales
+QUARTERS = 4
 
 
 class Place:
@@ -153,15 +147,223 @@
     return jnp.where(row == 2, third, out)
 
 
-def head_kernel(
-    final_ref, targets_ref, weight_hbm, logits_hbm, norms_ref,
-    g, weight, logits, halves, stats, by_group, by_section, merged, solved,
-    weight_sem, out_sem, swap_send, swap_recv, ring_send, ring_recv, pair_send, pair_recv,
+def one_hot(table, tokens):
+    shape = (tokens, 256)
+    column = lax.broadcasted_iota(jnp.int32, shape, 1)
+    token = lax.broadcasted_iota(jnp.int32, shape, 0)
+    expert = lax.div(column, 16).astype(jnp.float32)
+    slot = lax.rem(lax.div(column, 4), 2).astype(jnp.float32)
+    same = lax.rem(lax.div(column, 8), 2) == lax.div(token, 8)
+    piece = lax.rem(column, 4)
+    hits = [jnp.where(table[:, k : k + 1] == expert, 1.0, 0.0) for k in (0, 1)]
+    later = lax.broadcasted_iota(jnp.int32, (tokens, tokens), 0)
+    sooner = lax.broadcasted_iota(jnp.int32, (tokens, tokens), 1)
+    before = jnp.where((sooner < later) & (lax.div(sooner, 8) == lax.div(later, 8)), 1.0, 0.0)
+    earlier = jnp.dot(
+        before.astype(jnp.bfloat16), (hits[0] + hits[1]).astype(jnp.bfloat16), preferred_element_type=jnp.float32
+    )
+    placed = [jnp.where(same & (earlier == slot), hit, 0.0) for hit in hits]
+    return [
+        jnp.concatenate([jnp.where(piece == j, one, 0.0) for j in range(QUARTERS)], axis=0) for one in placed
+    ]
+
+
+def stack(values):
+    return jnp.concatenate([values[:, j * 256 : (j + 1) * 256] for j in range(QUARTERS)], axis=0)
+
+
+def experts(
+    where, hidden_ref, routes_ref, gates_ref, gain_ref, final_gain_ref, weight_in, weight_out, loads, g,
+    pack, outgoing, incoming, rows, units, away, sent_half, near, summed, parts, returning, returned, spread,
+    pack_send, pack_recv, go_send, go_recv, row_send, row_recv, rowp_send, rowp_recv, half_send, half_recv,
+    sum_send, sum_recv, back_send, back_recv, ln_send, ln_recv,
+):
+    core, m = where.core, where.y * 2 + where.zl
+    mine = pl.ds(pl.multiple_of(core * HALF, HALF), HALF)
+    theirs = pl.ds(pl.multiple_of((1 - core) * HALF, HALF), HALF)
+    to_expert = lambda other: (where.s, other)
+    to_chip = lambda other: ((lax.rem(other, 2) * 4 + lax.div(other, 2)) * 2 + core, where.e)
+    features = 2 * HALF
+
+    lane = lax.broadcasted_iota(jnp.int32, (8, 128), 1)
+    routes = routes_ref[...].astype(jnp.float32)
+    gates = gates_ref[...]
+    table = jnp.where(lane == 0, routes[:, 0:1], jnp.where(lane == 1, routes[:, 1:2], 0.0))
+    table = jnp.where(lane == 2, gates[:, 0:1], jnp.where(lane == 3, gates[:, 1:2], table))
+    pack[core, :, 0:features] = hidden_ref[...].astype(jnp.float32)
+    pack[core, :, features:] = table
+    swap = remote(pack.at[core], pack.at[core], pack_send, pack_recv, where.sibling)
+    swap.start()
+    swap.wait()
+
+    tokens = 16
+    whole = pack[:, :, 0:features].reshape(tokens, features)
+    table = pack[:, :, features:].reshape(tokens, 128)
+    average = jnp.mean(whole, axis=-1, keepdims=True)
+    centered = whole - average
+    spread_of = jnp.mean(centered * centered, axis=-1, keepdims=True)
+    residual = pack[:, :, mine].reshape(tokens, HALF)
+    normed = ((residual - average) * lax.rsqrt(spread_of + 1e-05) * gain_ref[:, mine]).astype(jnp.bfloat16)
+    chosen = one_hot(table, tokens)
+    place = jnp.transpose(chosen[0] + chosen[1]).astype(jnp.bfloat16)
+    slots = jnp.dot(place, stack(normed), preferred_element_type=jnp.float32).astype(jnp.bfloat16)
+    outgoing[...] = slots.reshape(16, 16, 256)
+    incoming[where.e] = outgoing[where.e]
+    exchange(16, where.e, to_expert, lambda other: outgoing.at[other], incoming, go_send, go_recv)
+
+    down = lax.broadcasted_iota(jnp.int32, (256, 256), 0)
+    across = lax.broadcasted_iota(jnp.int32, (256, 256), 1)
+    split = jnp.where(across == 4 * lax.rem(down, 64) + lax.div(down, 64), 1.0, 0.0).astype(jnp.bfloat16)
+    join = jnp.where(down == 4 * lax.rem(across, 64) + lax.div(across, 64), 1.0, 0.0).astype(jnp.bfloat16)
+    arrived = jnp.dot(split, incoming[...].reshape(256, 256), preferred_element_type=jnp.float32)
+    for j in range(QUARTERS):
+        rows[core, m, :, j * 256 : (j + 1) * 256] = arrived[j * 64 : (j + 1) * 64].astype(jnp.bfloat16)
+
+    own = rows.at[core, m]
+    pair = lambda i, block: remote(block, block, rowp_send.at[i], rowp_recv.at[i], where.sibling)
+    pair(0, own).start()
+
+    def send_rows(i, _):
+        remote(own, own, row_send.at[i], row_recv.at[i], to_chip(lax.rem(m + i, 8))).start()
+        return 0
+
+    def take_rows(i, _):
+        origin = lax.rem(m - i + 8, 8)
+        block = rows.at[core, origin]
+        remote(block, block, row_send.at[i], row_recv.at[i], to_chip(origin)).wait_recv()
+        pair(i, block).start()
+        return 0
+
+    def take_pair(i, _):
+        pair(i, rows.at[1 - core, lax.rem(m - i + 8, 8)]).wait_recv()
+        return 0
+
+    def rows_left(i, _):
+        remote(own, own, row_send.at[i], row_recv.at[i], to_chip(lax.rem(m + i, 8))).wait_send()
+        return 0
+
+    def pairs_left(i, _):
+        pair(i, own).wait_send()
+        return 0
+
+    lax.fori_loop(1, 8, send_rows, 0)
+    lax.fori_loop(1, 8, take_rows, 0)
+    lax.fori_loop(0, 8, take_pair, 0)
+
+    loads[0].wait()
+    loads[1].wait()
+
+    def first(i, _):
+        low = rows[0, pl.ds(i * 4, 4)].reshape(256, HALF)
+        high = rows[1, pl.ds(i * 4, 4)].reshape(256, HALF)
+        found = jnp.dot(low, weight_in[0:HALF], preferred_element_type=jnp.float32)
+        found = found + jnp.dot(high, weight_in[HALF:], preferred_element_type=jnp.float32)
+        units[pl.ds(i * 2, 2)] = jnp.maximum(found, 0.0).astype(jnp.bfloat16).reshape(2, 128, -1)
+        return 0
+
+    lax.fori_loop(0, 2, first, 0)
+
+    def half(i, other):
+        return remote(away.at[other], sent_half.at[other], half_send.at[i], half_recv.at[i], where.sibling)
+
+    def second(i, _):
+        other = lax.rem(where.y + 1 + i, 4)
+        some = units[other]
+        away[other] = jnp.dot(some, weight_out[:, theirs], preferred_element_type=jnp.float32).astype(jnp.bfloat16)
+        half(i, other).start()
+        near[other] = jnp.dot(some, weight_out[:, mine], preferred_element_type=jnp.float32)
+        return 0
+
+    lax.fori_loop(0, 4, second, 0)
+
+    def part(block, origin):
+        return remote(summed.at[block], parts.at[origin], sum_send.at[block], sum_recv.at[origin], to_chip(block))
+
+    def add(i, _):
+        other = lax.rem(where.y + 1 + i, 4)
+        half(i, other).wait_recv()
+        total = (near[other] + sent_half[other].astype(jnp.float32)).astype(jnp.bfloat16)
+        summed[pl.ds(other * 2, 2)] = total.reshape(2, 64, HALF)
+        for side in (0, 1):
+            block = other * 2 + side
+
+            @pl.when(block != m)
+            def _():
+                part(block, m).start()
+
+        return 0
+
+    lax.fori_loop(0, 4, add, 0)
+    parts[m] = summed[m]
+
+    def take_part(i, _):
+        origin = lax.rem(m - i + 8, 8)
+        remote(summed.at[origin], parts.at[origin], sum_send.at[origin], sum_recv.at[origin], to_chip(origin)).wait_recv()
+        return 0
+
+    lax.fori_loop(1, 8, take_part, 0)
+    total = parts[0].astype(jnp.float32)
+    for i in range(1, 8):
+        total = total + parts[i].astype(jnp.float32)
+    results = jnp.dot(join, stack(total.astype(jnp.bfloat16)), preferred_element_type=jnp.float32)
+    returning[...] = results.astype(jnp.bfloat16).reshape(16, 16, 256)
+    returned[where.e] = returning[where.e]
+    exchange(16, where.e, to_expert, lambda other: returning.at[other], returned, back_send, back_recv)
+
+    back = returned[...].reshape(256, 256)
+    mixed = [residual[:, j * 256 : (j + 1) * 256] for j in range(QUARTERS)]
+    for k in (0, 1):
+        found = jnp.dot(chosen[k].astype(jnp.bfloat16), back, preferred_element_type=jnp.float32)
+        gate = table[:, 2 + k : 3 + k]
+        mixed = [old + gate * found[j * tokens : (j + 1) * tokens] for j, old in enumerate(mixed)]
+    mixed = jnp.concatenate(mixed, axis=1)
+    center = jnp.mean(mixed, axis=-1, keepdims=True)
+    squares = jnp.sum((mixed - center) * (mixed - center), axis=-1, keepdims=True)
+    lane = lax.broadcasted_iota(jnp.int32, (tokens, 128), 1)
+    spread[core] = jnp.where(lane == 0, center, jnp.where(lane == 1, squares, 0.0))
+    swap = remote(spread.at[core], spread.at[core], ln_send, ln_recv, where.sibling)
+    swap.start()
+    swap.wait()
+    centers = [spread[i, :, 0:1] for i in (0, 1)]
+    average = 0.5 * (centers[0] + centers[1])
+    apart = centers[0] - centers[1]
+    variance = (spread[0, :, 1:2] + spread[1, :, 1:2] + apart * apart * (0.5 * HALF)) / features
+    final = (mixed - average) * lax.rsqrt(variance + 1e-05) * final_gain_ref[:, mine]
+    g[core, where.zl, where.y, where.x, where.zh] = final.astype(jnp.bfloat16)
+
+    lax.fori_loop(1, 8, rows_left, 0)
+    lax.fori_loop(0, 8, pairs_left, 0)
+
+    def halves_left(i, _):
+        half(i, lax.rem(where.y + 1 + i, 4)).wait_send()
+        return 0
+
+    lax.fori_loop(0, 4, halves_left, 0)
+
+    def parts_left(i, _):
+        part(lax.rem(m + i, 8), m).wait_send()
+        return 0
+
+    lax.fori_loop(1, 8, parts_left, 0)
+
+
+def layer_kernel(
+    hidden_ref, routes_ref, gates_ref, gain_ref, final_gain_ref, targets_ref, in_hbm, out_hbm, weight_hbm,
+    logits_hbm, norms_ref,
+    g, weight, logits, stats, by_group, by_section, merged, solved,
+    weight_sem, out_sem, ring_send, ring_recv, pair_send, pair_recv,
     one_send, one_recv, two_send, two_recv, three_send, three_recv,
+    weight_in, weight_out, weight_sems, *scratch,
 ):
     where = Place()
     barrier = pltpu.get_barrier_semaphore()
     load = pltpu.make_async_copy(weight_hbm, weight, weight_sem)
+    loads = [
+        pltpu.make_async_copy(in_hbm.at[0], weight_in, weight_sems.at[0]),
+        pltpu.make_async_copy(out_hbm.at[0], weight_out, weight_sems.at[1]),
+    ]
+    for one in loads:
+        one.start()
     load.start()
 
     def greet(i, _):
@@ -178,17 +380,13 @@
         pl.semaphore_signal(barrier, inc=1, device_id=where.beside("z", step), device_id_type=MESH)
     pl.semaphore_wait(barrier, 32)
 
+    experts(
+        where, hidden_ref, routes_ref, gates_ref, gain_ref, final_gain_ref, weight_in, weight_out, loads, g, *scratch
+    )
     for core in (0, 1):
 
         @pl.when(where.core == core)
         def _():
-            away = final_ref.at[:, pl.ds((1 - core) * HALF, HALF)]
-            swap = remote(away, halves, swap_send, swap_recv, where.sibling)
-            swap.start()
-            swap.wait()
-            mine = final_ref[:, core * HALF : (core + 1) * HALF]
-            both = (mine, halves[...]) if core == 0 else (halves[...], mine)
-            g[core, where.zl, where.y, where.x, where.zh] = jnp.concatenate(both, axis=0).astype(jnp.bfloat16)
             gather(core, where, g, ring_send, ring_recv, pair_send, pair_recv)
 
     load.wait()
@@ -246,41 +444,57 @@
     lax.fori_loop(0, PIECES, stored, 0)
 
 
-def head(final, targets, weight):
+def layer(hidden, routes, gates, gain, final_gain, targets, weight_in, weight_out, weight):
     features, columns = weight.shape
     tokens = targets.size
+    inner = weight_in.shape[2]
     dma = pltpu.SemaphoreType.DMA
+    bf16, f32 = jnp.bfloat16, jnp.float32
+    vmem, hbm = pl.BlockSpec(memory_space=pltpu.VMEM), pl.BlockSpec(memory_space=pl.ANY)
     return pl.pallas_call(
-        head_kernel,
-        name="head",
+        layer_kernel,
+        name="layer",
         out_shape=(
-            jax.ShapeDtypeStruct((tokens, columns), jnp.float32),
-            jax.ShapeDtypeStruct((16, 8, 128), jnp.float32),
+            jax.ShapeDtypeStruct((tokens, columns), f32),
+            jax.ShapeDtypeStruct((16, 8, 128), f32),
         ),
-        in_specs=[
-            pl.BlockSpec(memory_space=pltpu.VMEM),
-            pl.BlockSpec(memory_space=pltpu.VMEM),
-            pl.BlockSpec(memory_space=pl.ANY),
-        ],
-        out_specs=(pl.BlockSpec(memory_space=pl.ANY), pl.BlockSpec(memory_space=pltpu.VMEM)),
+        in_specs=[vmem] * 6 + [hbm] * 3,
+        out_specs=(hbm, vmem),
         scratch_shapes=[
-            pltpu.VMEM((2, 2, 4, 4, 4, 16, HALF), jnp.bfloat16),
-            pltpu.VMEM((features, columns), jnp.bfloat16),
-            pltpu.VMEM((tokens, columns), jnp.float32),
-            pltpu.VMEM((8, HALF), jnp.float32),
-            pltpu.VMEM((16, 8, 128), jnp.float32),
-            pltpu.VMEM((16, 8, 128), jnp.float32),
-            pltpu.VMEM((16, 8, 128), jnp.float32),
-            pltpu.VMEM((8, 128), jnp.float32),
-            pltpu.VMEM((8, 128), jnp.float32),
-            dma, dma((PIECES,)), dma, dma,
+            pltpu.VMEM((2, 2, 4, 4, 4, 16, HALF), bf16),
+            pltpu.VMEM((features, columns), bf16),
+            pltpu.VMEM((tokens, columns), f32),
+            pltpu.VMEM((16, 8, 128), f32),
+            pltpu.VMEM((16, 8, 128), f32),
+            pltpu.VMEM((16, 8, 128), f32),
+            pltpu.VMEM((8, 128), f32),
+            pltpu.VMEM((8, 128), f32),
+            dma, dma((PIECES,)),
             dma((16,)), dma((16,)), dma((17,)), dma((17,)),
             dma((16,)), dma((16,)), dma((16,)), dma((16,)), dma((16,)), dma((16,)),
+            pltpu.VMEM((features, inner), bf16),
+            pltpu.VMEM((inner, features), bf16),
+            dma((2,)),
+            pltpu.VMEM((2, 8, features + 128), f32),
+            pltpu.VMEM((16, 16, 256), bf16),
+            pltpu.VMEM((16, 16, 256), bf16),
+            pltpu.VMEM((2, 8, 64, HALF), bf16),
+            pltpu.VMEM((4, 128, inner), bf16),
+            pltpu.VMEM((4, 128, HALF), bf16),
+            pltpu.VMEM((4, 128, HALF), bf16),
+            pltpu.VMEM((4, 128, HALF), f32),
+            pltpu.VMEM((8, 64, HALF), bf16),
+            pltpu.VMEM((8, 64, HALF), bf16),
+            pltpu.VMEM((16, 16, 256), bf16),
+            pltpu.VMEM((16, 16, 256), bf16),
+            pltpu.VMEM((2, 16, 128), f32),
+            dma, dma, dma((16,)), dma((16,)), dma((8,)), dma((8,)), dma((8,)), dma((8,)),
+            dma((4,)), dma((4,)), dma((8,)), dma((8,)), dma((16,)), dma((16,)), dma, dma,
         ],
         compiler_params=pltpu.CompilerParams(
-            collective_id=1, has_side_effects=True, vmem_limit_bytes=48 * 1024 * 1024
+            collective_id=1, has_side_effects=True, vmem_limit_bytes=56 * 1024 * 1024
         ),
-    )(final, targets, weight)
+    )(hidden, routes, gates, gain, final_gain, targets, weight_in, weight_out, weight)
 
 
 def finish_kernel(logits_ref, norms_ref, lengths_ref, probs_ref, head_ref, loss_ref):
@@ -321,47 +535,10 @@
 def on_device(
     hidden, routes, gates, targets, target_lengths, moe_gain, fc_in, fc_out, final_gain, head_weight
 ):
-    token_rows = hidden.shape[0]
-    features = hidden.shape[1]
-    groups = lax.axis_size("expert")
-    capacity = max(2, (3 * token_rows + groups - 1) // groups)
-    residual = hidden.astype(jnp.float32)
-    normed = layer_norm(residual, moe_gain).astype(jnp.bfloat16)
-    flat_routes = routes.reshape(-1)
-    labels = jnp.arange(groups, dtype=jnp.int32)
-    matches = (flat_routes[:, None] == labels[None, :]).astype(jnp.int32)
-    earlier = jnp.cumsum(matches, axis=0) - matches
-    slot_index = jnp.sum(earlier * matches, axis=1)
-    placement = flat_routes * capacity + slot_index
-    copies = jnp.repeat(normed, 2, axis=0)
-    outgoing = jnp.zeros((groups * capacity, features), jnp.bfloat16).at[placement].set(copies)
-    outgoing = outgoing.reshape(groups, capacity, features)
-    weight_in = fc_in[0]
-    weight_out = fc_out[0]
-    block_rows = lax.all_gather(
-        lax.all_to_all(outgoing, "expert", split_axis=0, concat_axis=0, tiled=True),
-        "section",
-        axis=0,
-        tiled=True,
+    wanted = targets.astype(jnp.float32).reshape(-1, TGT)
+    logits, norms = layer(
+        hidden, routes, gates, moe_gain[None], final_gain[None], wanted, fc_in, fc_out, head_weight
     )
-    sources = block_rows.shape[0]
-    slot_count = block_rows.shape[1]
-    flattened = block_rows.reshape(sources * slot_count, features)
-    hidden_units = jnp.maximum(
-        jnp.dot(flattened, weight_in, preferred_element_type=jnp.float32), 0.0
-    ).astype(jnp.bfloat16)
-    partial_value = jnp.dot(hidden_units, weight_out, preferred_element_type=jnp.float32)
-    partials = partial_value.reshape(sources, slot_count, features)
-    summed = lax.psum_scatter(
-        partials.astype(jnp.bfloat16), "section", scatter_dimension=0, tiled=True
-    )
-    returned_rows = lax.all_to_all(summed, "expert", split_axis=0, concat_axis=0, tiled=True)
-    results = returned_rows.reshape(groups * capacity, features)[placement]
-    results = results.astype(jnp.float32).reshape(token_rows, 2, features)
-    mixed = residual + gates[:, 0:1] * results[:, 0] + gates[:, 1:2] * results[:, 1]
-    final = layer_norm(mixed, final_gain).astype(jnp.bfloat16)
-    wanted = targets.astype(jnp.float32).reshape(-1, TGT)
-    logits, norms = head(final.astype(jnp.float32), wanted, head_weight)
     log_probs, head_logits, loss = finish(logits, norms, target_lengths)
     return (log_probs, head_logits, loss.reshape(-1))
 

time: 267 us -> 156 us (0.58)
  waiting for transfers between devices: 105 us -> 0 us
  Pallas kernels: 94.9 us -> 151 us
  blocking collectives: 21 us -> 0 us
  between operations: 14.2 us -> 0.64 us
  local copies, waits for them, and re-layouts: 11.8 us -> 2.69 us
  starting transfers between devices: 9.06 us -> 0 us
  matrix products: 6.05 us -> 0 us
  other arithmetic: 4.34 us -> 1.3 us
    reduce_scatter x1 -> x0, waiting for transfers between devices: 61.6 us -> none  [on_device(): lax.psum_scatter(partials.astype(jnp.bfloat16), 'section', scatter_dimens...]
    pallas_call x1, Pallas kernels: 84.1 us -> 140 us  [layer(): pl.pallas_call(layer_kernel, name='layer', out_shape=(jax.ShapeDtypeStruc...]
    all_gather x1 -> x0, waiting for transfers between devices: 33.5 us -> none  [on_device(): lax.all_gather(lax.all_to_all(outgoing, 'expert', split_axis=0, concat_ax...]
    all_to_all x1 -> x0, blocking collectives: 21 us -> none  [on_device(): lax.all_to_all(outgoing, 'expert', split_axis=0, concat_axis=0, tiled=True)]
    all_to_all x1 -> x0, waiting for transfers between devices: 9.47 us -> none  [on_device(): lax.all_to_all(summed, 'expert', split_axis=0, concat_axis=0, tiled=True)]
    all_to_all x1 -> x0, starting transfers between devices: 8.98 us -> none  [on_device(): lax.all_to_all(summed, 'expert', split_axis=0, concat_axis=0, tiled=True)]
    dot_general x2 -> x0, matrix products: 6.05 us -> none  [the longest x1 3.47 us: on_device(): jnp.dot(flattened, weight_in, preferred_element_type=jnp.float32)]
    reshape x4 -> x0, local copies, waits for them, and re-layouts: 4.28 us -> none  [the longest x1 4.1 us: on_device(): flattened = block_rows.reshape(sources * slot_count, features)]
  transfers between devices with their start and end apart: 3 -> 0, of which waited for: 3 -> 0; matrix products, arithmetic and copies ran while one was open for 0% -> 0% of each run, Pallas kernels for 0% -> 0%
where the time goes in v2:
time: 156 us
  Pallas kernels  151 us (97%)
  local copies, waits for them, and re-layouts  2.69 us (2%)
    pallas_call x1, Pallas kernels, layer(): pl.pallas_call(layer_kernel, name='layer', out_shape=(jax.ShapeDtypeStruc...  140 us
    pallas_call x1, Pallas kernels, finish(): pl.pallas_call(finish_kernel, name='finish', grid=(groups,), out_shape=(j...  10.7 us

profile of v2, /device:TPU:1, one launch (start us, length us, event | category | flops | bytes accessed | tf_op | source)
XLA Modules:
  0.0 155.6 jit_solution(5870829994352462189)
XLA Ops:
  0.6 1.3 copy.13.routes_ref
  2.0 1.3 copy.14.gates_ref
  3.3 1.3 convert_bitcast_fusion.targets_ref
  4.6 140.2 %layer.1 = (f32[2048,640]{1,0:T(8,128)}, f32[16,8,128]{2,1,0:T(8,128)}) custom-call(bf16[8,2048]{1,0:T(8,128)(2,1)} %hidden_ref.1, s32[8,2]{1,0:T(8,128)} %copy.13.routes_ref, f32[8,2]{1,0:T(8,128)} %copy.14.gates_ref, f32[1,2048]{1,0:T(1,128)} %bitcast.5, f32[1,2048]{1,0:T(1,128)} %bitcast.6, f32[16,128]{1,0:T(8,128)} %convert_bitcast_fusion.targets_ref, ...), custom_call_target="tpu_custom_call" | custom-call | tf_op jit(solution)/shard_map/layer/pallas_call | solution.py:454
  144.8 10.7 %finish.1 = (bf16[2048,640]{1,0:T(8,128)(2,1)}, bf16[2048,640]{1,0:T(8,128)(2,1)}, f32[16,128]{1,0:T(8,128)}) custom-call(f32[2048,640]{1,0:T(8,128)} %get-tuple-element.8.logits_ref, f32[16,8,128]{2,1,0:T(8,128)} %get-tuple-element.9.norms_ref, s32[16]{0:T(128)} %lengths_ref.1), custom_call_target="tpu_custom_call" | custom-call | tf_op jit(solution)/shard_map/finish/pallas_call | solution.py:517

commit v3 on v2

--- a/solution.py
+++ b/solution.py
@@ -10,6 +10,7 @@
 HALF = 1024
 PIECES = 8
 QUARTERS = 4
+FINISH = 4
 
 
 class Place:
@@ -44,74 +45,156 @@
     )
 
 
-ORDERS = ((("x", 4), ("y", 4), ("z", 8)), (("z", 8), ("x", 4), ("y", 4)))
-
-
-def view(g, core, phase, where, pos, part):
-    lanes = slice(None) if part is None else pl.ds(part * (HALF // 2), HALF // 2)
-    if core == 0:
-        if phase == 0:
-            return g.at[0, where.zl, where.y, pos, where.zh, :, lanes]
-        if phase == 1:
-            return g.at[0, where.zl, pos, :, where.zh, :, lanes]
-        return g.at[0, lax.rem(pos, 2), :, :, lax.div(pos, 2), :, lanes]
-    if phase == 0:
-        return g.at[1, lax.rem(pos, 2), where.y, where.x, lax.div(pos, 2), :, lanes]
-    if phase == 1:
-        return g.at[1, :, where.y, pos, :, :, lanes]
-    return g.at[1, :, pos, :, :, :, lanes]
-
-
-def arrivals(g, core, where):
-    for phase, (axis, n) in enumerate(ORDERS[core]):
-        me = where.at(axis)
-        for step in range(1, n // 2 + 1):
-            last = step == n // 2
-            parts = (0, 1) if last else (None, None)
-            sends = (
-                view(g, core, phase, where, lax.rem(me - step + 1 + n, n), parts[0]),
-                view(g, core, phase, where, lax.rem(me + step - 1, n), parts[1]),
-            )
-            lands = (
-                view(g, core, phase, where, lax.rem(me - step + n, n), parts[0]),
-                view(g, core, phase, where, lax.rem(me + step, n), parts[1]),
-            )
-            yield axis, sends, lands
-
-
-def gather(core, where, g, ring_send, ring_recv, pair_send, pair_recv):
-    own = g.at[core, where.zl, where.y, where.x, where.zh]
-    shared = [(own, remote(own, own, pair_send.at[0], pair_recv.at[0], where.sibling))]
-    shared[0][1].start()
-    sent = []
-    k = 0
-    for axis, sends, lands in arrivals(g, core, where):
-        for side in (0, 1):
-            to = where.beside(axis, 1 - 2 * side)
-            copy = remote(sends[side], sends[side], ring_send.at[k + side], ring_recv.at[k + side], to)
-            copy.start()
-            sent.append(copy)
-        for side in (0, 1):
-            landed = lands[side]
-            remote(
-                landed, landed, ring_send.at[k + side], ring_recv.at[k + side], where.beside(axis, 2 * side - 1)
-            ).wait_recv()
-            copy = remote(landed, landed, pair_send.at[1 + k + side], pair_recv.at[1 + k + side], where.sibling)
-            copy.start()
-            shared.append((landed, copy))
-        k += 2
-    other = g.at[1 - core, where.zl, where.y, where.x, where.zh]
-    remote(other, other, pair_send.at[0], pair_recv.at[0], where.sibling).wait_recv()
-    k = 1
-    for _, _, lands in arrivals(g, 1 - core, where):
-        for side in (0, 1):
-            landed = lands[side]
-            remote(landed, landed, pair_send.at[k], pair_recv.at[k], where.sibling).wait_recv()
-            k += 1
-    for copy in sent:
-        copy.wait_send()
-    for _, copy in shared:
-        copy.wait_send()
+class Wires:
+    def __init__(self, send, recv):
+        self.send, self.recv, self.sent = send, recv, []
+
+    def push(self, src, dst, to):
+        k = len(self.sent)
+        copy = remote(src, dst, self.send.at[k], self.recv.at[k], to)
+        copy.start()
+        self.sent.append(copy)
+        return k
+
+    def pull(self, k, landed, origin):
+        remote(landed, landed, self.send.at[k], self.recv.at[k], origin).wait_recv()
+
+    def drain(self):
+        for copy in self.sent:
+            copy.wait_send()
+
+
+class Shared:
+    def __init__(self, where, wires):
+        self.where, self.wires, self.blocks = where, wires, []
+
+    def push(self, block):
+        mine = block(self.where.core)
+        self.blocks.append((self.wires.push(mine, mine, self.where.sibling), block))
+
+    def pull(self):
+        for k, block in self.blocks:
+            self.wires.pull(k, block(1 - self.where.core), self.where.sibling)
+
+
+def straight(where, wires, axis, n, block):
+    me = where.at(axis)
+    mine = block(where.core, me)
+    numbers = [wires.push(mine, mine, where.beside(axis, i)) for i in range(1, n)]
+    yield
+    for i, k in enumerate(numbers, 1):
+        wires.pull(k, block(where.core, lax.rem(me - i + n, n)), where.beside(axis, -i))
+
+
+def ring(where, wires, axis, n, block, shared=None):
+    me = where.at(axis)
+    for step in range(1, n // 2 + 1):
+        numbers = []
+        for side, sign in ((0, 1), (1, -1)):
+            part = side if step == n // 2 else None
+            mine = block(where.core, lax.rem(me - sign * (step - 1) + n, n), part)
+            numbers.append(wires.push(mine, mine, where.beside(axis, sign)))
+        yield
+        for side, sign in ((0, 1), (1, -1)):
+            part = side if step == n // 2 else None
+            pos = lax.rem(me - sign * step + n, n)
+            wires.pull(numbers[side], block(where.core, pos, part), where.beside(axis, -sign))
+            if shared is not None:
+                shared.push(lambda core, pos=pos, part=part: block(core, pos, part))
+
+
+def together(*chains):
+    chains = list(chains)
+    while chains:
+        chains = [chain for chain in chains if next(chain, chain) is not chain]
+
+
+def some(part, size):
+    return slice(None) if part is None else pl.ds(part * size, size)
+
+
+def gather(where, g, ring_send, ring_recv, pair_send, pair_recv):
+    wires, shared = Wires(ring_send, ring_recv), Shared(where, Wires(pair_send, pair_recv))
+    x, y, zl, zh = where.x, where.y, where.zl, where.zh
+    one, two, three, both = pl.ds(0, 384), pl.ds(384, 384), pl.ds(768, 256), pl.ds(384, 640)
+
+    def plane(core, pos, part=None):
+        return g.at[core, lax.rem(pos, 2), some(part, 2), :, lax.div(pos, 2), :, one]
+
+    def along_x(core, pos, part=None):
+        return g.at[core, some(part, 1), :, pos, :, :, two]
+
+    def along_y(core, pos, part=None):
+        return g.at[core, some(part, 1), pos, :, :, :, three]
+
+    def z_last():
+        yield from straight(where, wires, "x", 4, lambda core, pos: g.at[core, zl, y, pos, zh, :, one])
+        yield from straight(where, wires, "y", 4, lambda core, pos: g.at[core, zl, pos, :, zh, :, one])
+        shared.push(lambda core: plane(core, where.z))
+        yield from ring(where, wires, "z", 8, plane, shared)
+
+    def z_first():
+        return straight(
+            where, wires, "z", 8, lambda core, pos: g.at[core, lax.rem(pos, 2), y, x, lax.div(pos, 2), :, both]
+        )
+
+    def x_last():
+        yield from ring(
+            where, wires, "y", 4, lambda core, pos, part: g.at[core, some(part, 1), pos, x, :, :, two]
+        )
+        shared.push(lambda core: along_x(core, x))
+        yield from ring(where, wires, "x", 4, along_x, shared)
+
+    def y_last():
+        yield from ring(
+            where, wires, "x", 4, lambda core, pos, part: g.at[core, some(part, 1), y, pos, :, :, three]
+        )
+        shared.push(lambda core: along_y(core, y))
+        yield from ring(where, wires, "y", 4, along_y, shared)
+
+    def z_split():
+        yield from z_first()
+        chains = [x_last(), y_last()]
+        while chains:
+            chains = [chain for chain in chains if next(chain, chain) is not chain]
+            yield
+
+    together(z_last(), z_split())
+    shared.pull()
+    wires.drain()
+    shared.wires.drain()
+
+
+def spread_rows(where, rows, ring_send, ring_recv, pair_send, pair_recv):
+    wires, shared = Wires(ring_send, ring_recv), Shared(where, Wires(pair_send, pair_recv))
+    y, zl = where.y, where.zl
+    low, high = pl.ds(0, HALF // 2), pl.ds(HALF // 2, HALF // 2)
+    facing = ((((1 - zl) * 4 + y) * 2 + where.core), where.e)
+
+    def swap(block):
+        mine = block(where.core, zl)
+        k = wires.push(mine, mine, facing)
+        yield
+        wires.pull(k, block(where.core, 1 - zl), facing)
+
+    def z_last():
+        block = lambda core, side: rows.at[core, :, side, :, low]
+        yield from ring(
+            where, wires, "y", 4, lambda core, pos, part: rows.at[core, pos, zl, some(part, 32), low]
+        )
+        shared.push(lambda core: block(core, zl))
+        yield from swap(block)
+        shared.push(lambda core: block(core, 1 - zl))
+
+    def y_last():
+        block = lambda core, pos, part=None: rows.at[core, pos, some(part, 1), :, high]
+        yield from swap(lambda core, side: rows.at[core, y, side, :, high])
+        shared.push(lambda core: block(core, y))
+        yield from ring(where, wires, "y", 4, block, shared)
+
+    together(z_last(), y_last())
+    shared.pull()
+    return wires, shared.wires
 
 
 def exchange(n, me, to, src, dst, send, recv):
@@ -186,10 +269,12 @@
     features = 2 * HALF
 
     lane = lax.broadcasted_iota(jnp.int32, (8, 128), 1)
-    routes = routes_ref[...].astype(jnp.float32)
-    gates = gates_ref[...]
-    table = jnp.where(lane == 0, routes[:, 0:1], jnp.where(lane == 1, routes[:, 1:2], 0.0))
-    table = jnp.where(lane == 2, gates[:, 0:1], jnp.where(lane == 3, gates[:, 1:2], table))
+    same = lax.broadcasted_iota(jnp.int32, (8, 8), 0) == lax.broadcasted_iota(jnp.int32, (8, 8), 1)
+    table = jnp.zeros((8, 128), jnp.float32)
+    for place, (source, k) in enumerate(((routes_ref, 0), (routes_ref, 1), (gates_ref, 0), (gates_ref, 1))):
+        row = source[k : k + 1, :].astype(jnp.float32)
+        column = jnp.sum(jnp.where(same, row, 0.0), axis=1, keepdims=True)
+        table = jnp.where(lane == place, column, table)
     pack[core, :, 0:features] = hidden_ref[...].astype(jnp.float32)
     pack[core, :, features:] = table
     swap = remote(pack.at[core], pack.at[core], pack_send, pack_recv, where.sibling)
@@ -217,45 +302,15 @@
     join = jnp.where(down == 4 * lax.rem(across, 64) + lax.div(across, 64), 1.0, 0.0).astype(jnp.bfloat16)
     arrived = jnp.dot(split, incoming[...].reshape(256, 256), preferred_element_type=jnp.float32)
     for j in range(QUARTERS):
-        rows[core, m, :, j * 256 : (j + 1) * 256] = arrived[j * 64 : (j + 1) * 64].astype(jnp.bfloat16)
-
-    own = rows.at[core, m]
-    pair = lambda i, block: remote(block, block, rowp_send.at[i], rowp_recv.at[i], where.sibling)
-    pair(0, own).start()
-
-    def send_rows(i, _):
-        remote(own, own, row_send.at[i], row_recv.at[i], to_chip(lax.rem(m + i, 8))).start()
-        return 0
-
-    def take_rows(i, _):
-        origin = lax.rem(m - i + 8, 8)
-        block = rows.at[core, origin]
-        remote(block, block, row_send.at[i], row_recv.at[i], to_chip(origin)).wait_recv()
-        pair(i, block).start()
-        return 0
-
-    def take_pair(i, _):
-        pair(i, rows.at[1 - core, lax.rem(m - i + 8, 8)]).wait_recv()
-        return 0
-
-    def rows_left(i, _):
-        remote(own, own, row_send.at[i], row_recv.at[i], to_chip(lax.rem(m + i, 8))).wait_send()
-        return 0
-
-    def pairs_left(i, _):
-        pair(i, own).wait_send()
-        return 0
-
-    lax.fori_loop(1, 8, send_rows, 0)
-    lax.fori_loop(1, 8, take_rows, 0)
-    lax.fori_loop(0, 8, take_pair, 0)
-
+        rows[core, where.y, where.zl, :, j * 256 : (j + 1) * 256] = arrived[j * 64 : (j + 1) * 64].astype(jnp.bfloat16)
+
+    wires, pairs = spread_rows(where, rows, row_send, row_recv, rowp_send, rowp_recv)
     loads[0].wait()
     loads[1].wait()
 
     def first(i, _):
-        low = rows[0, pl.ds(i * 4, 4)].reshape(256, HALF)
-        high = rows[1, pl.ds(i * 4, 4)].reshape(256, HALF)
+        low = rows[0, pl.ds(i * 2, 2)].reshape(256, HALF)
+        high = rows[1, pl.ds(i * 2, 2)].reshape(256, HALF)
         found = jnp.dot(low, weight_in[0:HALF], preferred_element_type=jnp.float32)
         found = found + jnp.dot(high, weight_in[HALF:], preferred_element_type=jnp.float32)
         units[pl.ds(i * 2, 2)] = jnp.maximum(found, 0.0).astype(jnp.bfloat16).reshape(2, 128, -1)
@@ -331,8 +386,8 @@
     final = (mixed - average) * lax.rsqrt(variance + 1e-05) * final_gain_ref[:, mine]
     g[core, where.zl, where.y, where.x, where.zh] = final.astype(jnp.bfloat16)
 
-    lax.fori_loop(1, 8, rows_left, 0)
-    lax.fori_loop(0, 8, pairs_left, 0)
+    wires.drain()
+    pairs.drain()
 
     def halves_left(i, _):
         half(i, lax.rem(where.y + 1 + i, 4)).wait_send()
@@ -383,12 +438,7 @@
     experts(
         where, hidden_ref, routes_ref, gates_ref, gain_ref, final_gain_ref, weight_in, weight_out, loads, g, *scratch
     )
-    for core in (0, 1):
-
-        @pl.when(where.core == core)
-        def _():
-            gather(core, where, g, ring_send, ring_recv, pair_send, pair_recv)
-
+    gather(where, g, ring_send, ring_recv, pair_send, pair_recv)
     load.wait()
     columns = weight.shape[1]
     offset = (where.s * 16 + where.e) * columns
@@ -407,7 +457,7 @@
             logits[pl.ds(group * 128, 128), :] = part
             top = jnp.max(part, axis=1, keepdims=True)
             total = jnp.sum(jnp.exp(part - top), axis=1, keepdims=True)
-            wanted = jnp.transpose(jnp.broadcast_to(targets_ref[pl.ds(group, 1), :], (128, 128)))
+            wanted = jnp.transpose(jnp.broadcast_to(targets_ref[pl.ds(group, 1), :].astype(jnp.float32), (128, 128)))
             picked = jnp.zeros((128, 128), jnp.float32)
             for tile in range(columns // 128):
                 ids = (lane + (offset + tile * 128)).astype(jnp.float32)
@@ -470,7 +520,7 @@
             pltpu.VMEM((8, 128), f32),
             pltpu.VMEM((8, 128), f32),
             dma, dma((PIECES,)),
-            dma((16,)), dma((16,)), dma((17,)), dma((17,)),
+            dma((37,)), dma((37,)), dma((19,)), dma((19,)),
             dma((16,)), dma((16,)), dma((16,)), dma((16,)), dma((16,)), dma((16,)),
             pltpu.VMEM((features, inner), bf16),
             pltpu.VMEM((inner, features), bf16),
@@ -478,7 +528,7 @@
             pltpu.VMEM((2, 8, features + 128), f32),
             pltpu.VMEM((16, 16, 256), bf16),
             pltpu.VMEM((16, 16, 256), bf16),
-            pltpu.VMEM((2, 8, 64, HALF), bf16),
+            pltpu.VMEM((2, 4, 2, 64, HALF), bf16),
             pltpu.VMEM((4, 128, inner), bf16),
             pltpu.VMEM((4, 128, HALF), bf16),
             pltpu.VMEM((4, 128, HALF), bf16),
@@ -488,7 +538,7 @@
             pltpu.VMEM((16, 16, 256), bf16),
             pltpu.VMEM((16, 16, 256), bf16),
             pltpu.VMEM((2, 16, 128), f32),
-            dma, dma, dma((16,)), dma((16,)), dma((8,)), dma((8,)), dma((8,)), dma((8,)),
+            dma, dma, dma((16,)), dma((16,)), dma((10,)), dma((10,)), dma((7,)), dma((7,)),
             dma((4,)), dma((4,)), dma((8,)), dma((8,)), dma((16,)), dma((16,)), dma, dma,
         ],
         compiler_params=pltpu.CompilerParams(
@@ -498,26 +548,28 @@
 
 
 def finish_kernel(logits_ref, norms_ref, lengths_ref, probs_ref, head_ref, loss_ref):
-    values = logits_ref[...]
-    head_ref[...] = values.astype(jnp.bfloat16)
-    shift = jnp.transpose(jnp.broadcast_to(norms_ref[0, 0:1, :], (128, 128)))
-    for tile in range(values.shape[1] // 128):
-        lanes = slice(tile * 128, (tile + 1) * 128)
-        probs_ref[:, lanes] = (values[:, lanes] - shift).astype(jnp.bfloat16)
-
-    position = lax.broadcasted_iota(jnp.int32, (1, 128), 1)
-    group = pl.program_id(0)
-    loss_ref[pl.ds(group, 1), :] = jnp.where(position < lengths_ref[group], norms_ref[0, 1:2, :], 0.0)
+    step = pl.program_id(0)
+    position = lax.broadcasted_iota(jnp.int32, (1, TGT), 1)
+    for i in range(FINISH):
+        rows = slice(i * TGT, (i + 1) * TGT)
+        shift = jnp.transpose(jnp.broadcast_to(norms_ref[i, 0:1, :], (TGT, TGT)))
+        for tile in range(logits_ref.shape[1] // TGT):
+            lanes = slice(tile * TGT, (tile + 1) * TGT)
+            values = logits_ref[rows, lanes]
+            head_ref[rows, lanes] = values.astype(jnp.bfloat16)
+            probs_ref[rows, lanes] = (values - shift).astype(jnp.bfloat16)
+        group = step * FINISH + i
+        loss_ref[pl.ds(group, 1), :] = jnp.where(position < lengths_ref[group], norms_ref[i, 1:2, :], 0.0)
 
 
 def finish(logits, norms, lengths):
     tokens, columns = logits.shape
     groups = tokens // TGT
-    rows = pl.BlockSpec((TGT, columns), lambda i: (i, 0))
+    rows = pl.BlockSpec((FINISH * TGT, columns), lambda i: (i, 0))
     return pl.pallas_call(
         finish_kernel,
         name="finish",
-        grid=(groups,),
+        grid=(groups // FINISH,),
         out_shape=(
             jax.ShapeDtypeStruct((tokens, columns), jnp.bfloat16),
             jax.ShapeDtypeStruct((tokens, columns), jnp.bfloat16),
@@ -525,7 +577,7 @@
         ),
         in_specs=[
             rows,
-            pl.BlockSpec((1, 8, 128), lambda i: (i, 0, 0)),
+            pl.BlockSpec((FINISH, 8, 128), lambda i: (i, 0, 0)),
             pl.BlockSpec(memory_space=pltpu.SMEM),
         ],
         out_specs=(rows, rows, pl.BlockSpec((groups, TGT), lambda i: (0, 0))),
@@ -535,9 +587,9 @@
 def on_device(
     hidden, routes, gates, targets, target_lengths, moe_gain, fc_in, fc_out, final_gain, head_weight
 ):
-    wanted = targets.astype(jnp.float32).reshape(-1, TGT)
+    wanted = targets.reshape(-1, TGT)
     logits, norms = layer(
-        hidden, routes, gates, moe_gain[None], final_gain[None], wanted, fc_in, fc_out, head_weight
+        hidden, routes.T, gates.T, moe_gain[None], final_gain[None], wanted, fc_in, fc_out, head_weight
     )
     log_probs, head_logits, loss = finish(logits, norms, target_lengths)
     return (log_probs, head_logits, loss.reshape(-1))

time: 156 us -> 130 us (0.83)
  Pallas kernels: 151 us -> 129 us
  local copies, waits for them, and re-layouts: 2.69 us -> 0 us
    pallas_call x1, Pallas kernels: 140 us -> 124 us  [layer(): pl.pallas_call(layer_kernel, name='layer', out_shape=(jax.ShapeDtypeStruc...]
    pallas_call x1, Pallas kernels: 10.7 us -> 5.54 us  [finish(): pl.pallas_call(finish_kernel, name='finish', grid=(groups // FINISH,), ou...]
    unnamed x2 -> x0, local copies, waits for them, and re-layouts: 2.69 us -> none
where the time goes in v3:
time: 130 us
  Pallas kernels  129 us (99%)
    pallas_call x1, Pallas kernels, layer(): pl.pallas_call(layer_kernel, name='layer', out_shape=(jax.ShapeDtypeStruc...  124 us
    pallas_call x1, Pallas kernels, finish(): pl.pallas_call(finish_kernel, name='finish', grid=(groups // FINISH,), ou...  5.54 us

profile of v3, /device:TPU:1, one launch (start us, length us, event | category | flops | bytes accessed | tf_op | source)
XLA Modules:
  0.0 129.8 jit_solution(12564553092792301811)
XLA Ops:
  0.6 123.7 %layer.1 = (f32[2048,640]{1,0:T(8,128)}, f32[16,8,128]{2,1,0:T(8,128)}) custom-call(bf16[8,2048]{1,0:T(8,128)(2,1)} %hidden_ref.1, s32[2,8]{1,0:T(2,128)} %bitcast.9, f32[2,8]{1,0:T(2,128)} %bitcast.10, f32[1,2048]{1,0:T(1,128)} %bitcast.6, f32[1,2048]{1,0:T(1,128)} %bitcast.7, s32[16,128]{1,0:T(8,128)} %bitcast.8, bf16[1,2048,512]{2,1,0:T(8,128)(2,1)} %in_hbm.1, ...), custom_call_target="tpu_custom_call" | custom-call | tf_op jit(solution)/shard_map/layer/pallas_call | solution.py:504
  124.3 5.5 %finish.1 = (bf16[2048,640]{1,0:T(8,128)(2,1)}, bf16[2048,640]{1,0:T(8,128)(2,1)}, f32[16,128]{1,0:T(8,128)}) custom-call(f32[2048,640]{1,0:T(8,128)} %get-tuple-element.8.logits_ref, f32[16,8,128]{2,1,0:T(8,128)} %get-tuple-element.9.norms_ref, s32[16]{0:T(128)} %lengths_ref.1), custom_call_target="tpu_custom_call" | custom-call | tf_op jit(solution)/shard_map/finish/pallas_call | solution.py:569

commit v4 on v3

--- a/solution.py
+++ b/solution.py
@@ -10,7 +10,6 @@
 HALF = 1024
 PIECES = 8
 QUARTERS = 4
-FINISH = 4
 
 
 class Place:
@@ -75,6 +74,7 @@
     def pull(self):
         for k, block in self.blocks:
             self.wires.pull(k, block(1 - self.where.core), self.where.sibling)
+        self.blocks = []
 
 
 def straight(where, wires, axis, n, block):
@@ -113,54 +113,115 @@
     return slice(None) if part is None else pl.ds(part * size, size)
 
 
-def gather(where, g, ring_send, ring_recv, pair_send, pair_recv):
+def planes(where, wires, block, shared):
+    me = where.z
+    numbers = []
+    mine = block(where.core, me)
+    for step in (1, -1, 2, -2):
+        numbers.append((wires.push(mine, mine, where.beside("z", step)), step))
+    yield
+    for k, step in numbers:
+        pos = lax.rem(me - step + 8, 8)
+        wires.pull(k, block(where.core, pos), where.beside("z", -step))
+        shared.push(lambda core, pos=pos: block(core, pos))
+    numbers = []
+    for side, sign in ((0, 1), (1, -1)):
+        pos = lax.rem(me - 2 * sign + 8, 8)
+        for step, part in ((sign, None), (2 * sign, side)):
+            mine = block(where.core, pos, part)
+            numbers.append((wires.push(mine, mine, where.beside("z", step)), step, sign, part))
+    yield
+    for k, step, sign, part in numbers:
+        pos = lax.rem(me - step - 2 * sign + 8, 8)
+        wires.pull(k, block(where.core, pos, part), where.beside("z", -step))
+        shared.push(lambda core, pos=pos, part=part: block(core, pos, part))
+
+
+def gather(where, g, weight, logits, ring_send, ring_recv, pair_send, pair_recv):
     wires, shared = Wires(ring_send, ring_recv), Shared(where, Wires(pair_send, pair_recv))
     x, y, zl, zh = where.x, where.y, where.zl, where.zh
-    one, two, three, both = pl.ds(0, 384), pl.ds(384, 384), pl.ds(768, 256), pl.ds(384, 640)
-
-    def plane(core, pos, part=None):
-        return g.at[core, lax.rem(pos, 2), some(part, 2), :, lax.div(pos, 2), :, one]
-
-    def along_x(core, pos, part=None):
-        return g.at[core, some(part, 1), :, pos, :, :, two]
-
-    def along_y(core, pos, part=None):
-        return g.at[core, some(part, 1), pos, :, :, :, three]
-
-    def z_last():
-        yield from straight(where, wires, "x", 4, lambda core, pos: g.at[core, zl, y, pos, zh, :, one])
-        yield from straight(where, wires, "y", 4, lambda core, pos: g.at[core, zl, pos, :, zh, :, one])
-        shared.push(lambda core: plane(core, where.z))
-        yield from ring(where, wires, "z", 8, plane, shared)
-
-    def z_first():
-        return straight(
-            where, wires, "z", 8, lambda core, pos: g.at[core, lax.rem(pos, 2), y, x, lax.div(pos, 2), :, both]
-        )
-
-    def x_last():
-        yield from ring(
-            where, wires, "y", 4, lambda core, pos, part: g.at[core, some(part, 1), pos, x, :, :, two]
-        )
-        shared.push(lambda core: along_x(core, x))
-        yield from ring(where, wires, "x", 4, along_x, shared)
-
-    def y_last():
-        yield from ring(
-            where, wires, "x", 4, lambda core, pos, part: g.at[core, some(part, 1), y, pos, :, :, three]
-        )
-        shared.push(lambda core: along_y(core, y))
-        yield from ring(where, wires, "y", 4, along_y, shared)
-
-    def z_split():
-        yield from z_first()
-        chains = [x_last(), y_last()]
-        while chains:
-            chains = [chain for chain in chains if next(chain, chain) is not chain]
-            yield
-
-    together(z_last(), z_split())
+    one, two, three, rest = (0, 256), (256, 384), (640, 384), (256, 768)
+
+    def z_last(half):
+        def block(core, pos, part=None):
+            return g.at[
+                core, lax.rem(pos, 2), pl.ds(2 * half, 2), some(part, 2), lax.div(pos, 2), :, pl.ds(*one)
+            ]
+
+        shared.push(lambda core: block(core, where.z))
+        yield from planes(where, wires, block, shared)
+
+    def x_last(half):
+        def block(core, pos, part=None):
+            return g.at[core, half, some(part, 2), pos, :, :, pl.ds(*two)]
+
+        yield from straight(where, wires, "y", 4, lambda core, pos: g.at[core, half, pos, x, :, :, pl.ds(*two)])
+        shared.push(lambda core: block(core, x))
+        yield from ring(where, wires, "x", 4, block, shared)
+
+    def y_last(half):
+        def block(core, pos, part=None):
+            return g.at[core, half, pos, some(part, 2), :, :, pl.ds(*three)]
+
+        yield from straight(where, wires, "x", 4, lambda core, pos: g.at[core, half, y, pos, :, :, pl.ds(*three)])
+        shared.push(lambda core: block(core, y))
+        yield from ring(where, wires, "y", 4, block, shared)
+
+    def multiply(at, lanes):
+        start, width = lanes
+        total = logits[at]
+        shape = total.shape
+        total = total.reshape(256, shape[-1])
+        for core in (0, 1):
+            rows = g[(core, *at, slice(None), pl.ds(start, width))].reshape(256, width)
+            columns = weight[core * HALF + start : core * HALF + start + width]
+            total = total + jnp.dot(rows, columns, preferred_element_type=jnp.float32)
+        logits[at] = total.reshape(shape)
+
+    def over_planes(count, step):
+        def body(i, _):
+            pos = lax.rem(where.z + step(i), 8)
+            multiply((lax.rem(pos, 2), slice(None), slice(None), lax.div(pos, 2)), one)
+            return 0
+
+        lax.fori_loop(0, count, body, 0)
+
+    def over_slabs(count, step):
+        def body(i, _):
+            side, ahead = lax.rem(i, 2), step(lax.div(i, 2))
+            multiply((side, slice(None), lax.rem(x + ahead, 4), slice(None)), two)
+            multiply((side, lax.rem(y + ahead, 4), slice(None), slice(None)), three)
+            return 0
+
+        lax.fori_loop(0, 2 * count, body, 0)
+
+    def advance(chains):
+        for chain in chains:
+            next(chain, None)
+
+    by_x = straight(where, wires, "x", 4, lambda core, pos: g.at[core, zl, y, pos, zh, :, pl.ds(*one)])
+    by_y = straight(where, wires, "y", 4, lambda core, pos: g.at[core, zl, pos, :, zh, :, pl.ds(*one)])
+    by_z = straight(
+        where, wires, "z", 8, lambda core, pos: g.at[core, lax.rem(pos, 2), y, x, lax.div(pos, 2), :, pl.ds(*rest)]
+    )
+    early, late = [x_last(0), y_last(0)], [x_last(1), y_last(1)]
+    advance([by_x, by_z])
+    logits[...] = jnp.zeros_like(logits)
+    advance([by_x, by_y, by_z] + early + late)
+    advance([by_y])
+    early, late = [z_last(0)] + early, [z_last(1)] + late
+    advance(early + late)
     shared.pull()
+    over_planes(1, lambda i: 0)
+    over_slabs(1, lambda i: 0)
+    advance(early + late)
+    shared.pull()
+    over_planes(4, lambda i: i + 1 + 3 * lax.div(i, 2))
+    over_slabs(2, lambda i: 2 * i + 1)
+    advance(early + late)
+    shared.pull()
+    over_planes(3, lambda i: i + 3)
+    over_slabs(1, lambda i: 2)
     wires.drain()
     shared.wires.drain()
 
@@ -256,8 +317,8 @@
 
 
 def experts(
-    where, hidden_ref, routes_ref, gates_ref, gain_ref, final_gain_ref, weight_in, weight_out, loads, g,
-    pack, outgoing, incoming, rows, units, away, sent_half, near, summed, parts, returning, returned, spread,
+    where, barrier, small, late, hidden_ref, routes_ref, gates_ref, gain_ref, final_gain_ref, weight_in, weight_out, loads, g,
+    local, outbox, pack, outgoing, incoming, rows, units, away, sent_half, near, summed, parts, returning, returned, spread,
     pack_send, pack_recv, go_send, go_recv, row_send, row_recv, rowp_send, rowp_recv, half_send, half_recv,
     sum_send, sum_recv, back_send, back_recv, ln_send, ln_recv,
 ):
@@ -268,6 +329,8 @@
     to_chip = lambda other: ((lax.rem(other, 2) * 4 + lax.div(other, 2)) * 2 + core, where.e)
     features = 2 * HALF
 
+    for one in small:
+        one.wait()
     lane = lax.broadcasted_iota(jnp.int32, (8, 128), 1)
     same = lax.broadcasted_iota(jnp.int32, (8, 8), 0) == lax.broadcasted_iota(jnp.int32, (8, 8), 1)
     table = jnp.zeros((8, 128), jnp.float32)
@@ -275,20 +338,26 @@
         row = source[k : k + 1, :].astype(jnp.float32)
         column = jnp.sum(jnp.where(same, row, 0.0), axis=1, keepdims=True)
         table = jnp.where(lane == place, column, table)
-    pack[core, :, 0:features] = hidden_ref[...].astype(jnp.float32)
-    pack[core, :, features:] = table
-    swap = remote(pack.at[core], pack.at[core], pack_send, pack_recv, where.sibling)
-    swap.start()
-    swap.wait()
-
-    tokens = 16
-    whole = pack[:, :, 0:features].reshape(tokens, features)
-    table = pack[:, :, features:].reshape(tokens, 128)
+    whole = hidden_ref[...].astype(jnp.float32)
     average = jnp.mean(whole, axis=-1, keepdims=True)
     centered = whole - average
     spread_of = jnp.mean(centered * centered, axis=-1, keepdims=True)
-    residual = pack[:, :, mine].reshape(tokens, HALF)
-    normed = ((residual - average) * lax.rsqrt(spread_of + 1e-05) * gain_ref[:, mine]).astype(jnp.bfloat16)
+    normed = centered * lax.rsqrt(spread_of + 1e-05) * gain_ref[...]
+    local[0] = normed.astype(jnp.bfloat16).astype(jnp.float32)
+    local[1] = whole
+    for box, half in ((outbox, theirs), (pack.at[core], mine)):
+        box[:, 0:HALF] = local[0, :, half]
+        box[:, HALF:features] = local[1, :, half]
+        box[:, features:] = table
+    pl.semaphore_wait(barrier, 32)
+    swap = remote(outbox, pack.at[core], pack_send, pack_recv, where.sibling)
+    swap.start()
+    swap.wait()
+
+    tokens = 16
+    normed = pack[:, :, 0:HALF].reshape(tokens, HALF).astype(jnp.bfloat16)
+    residual = pack[:, :, HALF:features].reshape(tokens, HALF)
+    table = pack[:, :, features:].reshape(tokens, 128)
     chosen = one_hot(table, tokens)
     place = jnp.transpose(chosen[0] + chosen[1]).astype(jnp.bfloat16)
     slots = jnp.dot(place, stack(normed), preferred_element_type=jnp.float32).astype(jnp.bfloat16)
@@ -383,6 +452,7 @@
     average = 0.5 * (centers[0] + centers[1])
     apart = centers[0] - centers[1]
     variance = (spread[0, :, 1:2] + spread[1, :, 1:2] + apart * apart * (0.5 * HALF)) / features
+    late.wait()
     final = (mixed - average) * lax.rsqrt(variance + 1e-05) * final_gain_ref[:, mine]
     g[core, where.zl, where.y, where.x, where.zh] = final.astype(jnp.bfloat16)
 
@@ -403,15 +473,23 @@
 
 
 def layer_kernel(
-    hidden_ref, routes_ref, gates_ref, gain_ref, final_gain_ref, targets_ref, in_hbm, out_hbm, weight_hbm,
-    logits_hbm, norms_ref,
+    hidden_hbm, routes_hbm, gates_hbm, gain_hbm, final_gain_hbm, targets_hbm, in_hbm, out_hbm, weight_hbm,
+    kept, norms_ref,
     g, weight, logits, stats, by_group, by_section, merged, solved,
-    weight_sem, out_sem, ring_send, ring_recv, pair_send, pair_recv,
+    weight_sem, ring_send, ring_recv, pair_send, pair_recv,
     one_send, one_recv, two_send, two_recv, three_send, three_recv,
-    weight_in, weight_out, weight_sems, *scratch,
+    weight_in, weight_out, weight_sems, hidden_ref, routes_ref, gates_ref, gain_ref, final_gain_ref, targets_ref,
+    small_sems, *scratch,
 ):
     where = Place()
     barrier = pltpu.get_barrier_semaphore()
+    pairs = (
+        (hidden_hbm, hidden_ref), (routes_hbm, routes_ref), (gates_hbm, gates_ref), (gain_hbm, gain_ref),
+        (final_gain_hbm, final_gain_ref), (targets_hbm, targets_ref),
+    )
+    small = [pltpu.make_async_copy(a, b, small_sems.at[i]) for i, (a, b) in enumerate(pairs)]
+    for one in small:
+        one.start()
     load = pltpu.make_async_copy(weight_hbm, weight, weight_sem)
     loads = [
         pltpu.make_async_copy(in_hbm.at[0], weight_in, weight_sems.at[0]),
@@ -433,31 +511,31 @@
     lax.fori_loop(1, 16, greet, 0)
     for step in (1, -1):
         pl.semaphore_signal(barrier, inc=1, device_id=where.beside("z", step), device_id_type=MESH)
-    pl.semaphore_wait(barrier, 32)
 
     experts(
-        where, hidden_ref, routes_ref, gates_ref, gain_ref, final_gain_ref, weight_in, weight_out, loads, g, *scratch
+        where, barrier, small[:4], small[4], hidden_ref, routes_ref, gates_ref, gain_ref, final_gain_ref, weight_in, weight_out,
+        loads, g, *scratch
     )
-    gather(where, g, ring_send, ring_recv, pair_send, pair_recv)
     load.wait()
+    small[5].wait()
+    gather(where, g, weight, logits, ring_send, ring_recv, pair_send, pair_recv)
+
     columns = weight.shape[1]
     offset = (where.s * 16 + where.e) * columns
     lane = lax.broadcasted_iota(jnp.int32, (128, 128), 1)
 
     def chunk(i, _):
         zl, y = lax.div(i, 4), lax.rem(i, 4)
-        low = g[0, zl, y].reshape(256, HALF)
-        high = g[1, zl, y].reshape(256, HALF)
-        found = jnp.dot(low, weight[0:HALF], preferred_element_type=jnp.float32)
-        found = found + jnp.dot(high, weight[HALF:], preferred_element_type=jnp.float32)
-        found = found.reshape(16, 2, 8, columns)
         for core in (0, 1):
             group = i * 2 + core
-            part = found[:, core].reshape(128, columns)
-            logits[pl.ds(group * 128, 128), :] = part
+            part = logits[zl, y, :, :, core * 8 : (core + 1) * 8]
+            kept[group] = part
+            part = part.reshape(128, columns)
             top = jnp.max(part, axis=1, keepdims=True)
             total = jnp.sum(jnp.exp(part - top), axis=1, keepdims=True)
-            wanted = jnp.transpose(jnp.broadcast_to(targets_ref[pl.ds(group, 1), :].astype(jnp.float32), (128, 128)))
+            wanted = jnp.transpose(
+                jnp.broadcast_to(targets_ref[pl.ds(group, 1), :].astype(jnp.float32), (128, 128))
+            )
             picked = jnp.zeros((128, 128), jnp.float32)
             for tile in range(columns // 128):
                 ids = (lane + (offset + tile * 128)).astype(jnp.float32)
@@ -465,33 +543,22 @@
             picked = jnp.sum(picked, axis=1, keepdims=True)
             table = jnp.where(lane == 0, top, jnp.where(lane == 1, total, jnp.where(lane == 2, picked, 0.0)))
             stats[group] = jnp.transpose(table)[0:8]
-        pltpu.make_async_copy(
-            logits.at[pl.ds(i * 256, 256)], logits_hbm.at[pl.ds(i * 256, 256)], out_sem.at[i]
-        ).start()
         return 0
 
     lax.fori_loop(0, PIECES, chunk, 0)
 
     to_expert = lambda other: (where.s, other)
     to_section = lambda other: (other, where.e)
-    by_group[where.e] = stats[where.e]
-    exchange(16, where.e, to_expert, lambda other: stats.at[other], by_group, one_send, one_recv)
+    by_group[where.s] = stats[where.s]
+    exchange(16, where.s, to_section, lambda other: stats.at[other], by_group, one_send, one_recv)
     merged[...] = rows8(*merge(by_group[...]))
-    by_section[where.s] = merged[...]
-    exchange(16, where.s, to_section, lambda other: merged, by_section, two_send, two_recv)
+    by_section[where.e] = merged[...]
+    exchange(16, where.e, to_expert, lambda other: merged, by_section, two_send, two_recv)
     top, total, picked = merge(by_section[...])
     log_norm = top + jnp.log(total)
     solved[...] = rows8(log_norm, log_norm - picked, jnp.zeros_like(picked))
-    norms_ref[where.e] = solved[...]
-    exchange(16, where.e, to_expert, lambda other: solved, norms_ref, three_send, three_recv)
-
-    def stored(i, _):
-        pltpu.make_async_copy(
-            logits.at[pl.ds(i * 256, 256)], logits_hbm.at[pl.ds(i * 256, 256)], out_sem.at[i]
-        ).wait()
-        return 0
-
-    lax.fori_loop(0, PIECES, stored, 0)
+    norms_ref[where.s] = solved[...]
+    exchange(16, where.s, to_section, lambda other: solved, norms_ref, three_send, three_recv)
 
 
 def layer(hidden, routes, gates, gain, final_gain, targets, weight_in, weight_out, weight):
@@ -500,31 +567,41 @@
     inner = weight_in.shape[2]
     dma = pltpu.SemaphoreType.DMA
     bf16, f32 = jnp.bfloat16, jnp.float32
-    vmem, hbm = pl.BlockSpec(memory_space=pltpu.VMEM), pl.BlockSpec(memory_space=pl.ANY)
+    vmem = pl.BlockSpec(memory_space=pltpu.VMEM)
+    operands = (hidden, routes, gates, gain, final_gain, targets, weight_in, weight_out, weight)
     return pl.pallas_call(
         layer_kernel,
         name="layer",
         out_shape=(
-            jax.ShapeDtypeStruct((tokens, columns), f32),
+            pltpu.VMEM((16, 4, 4, 8, columns), f32),
             jax.ShapeDtypeStruct((16, 8, 128), f32),
         ),
-        in_specs=[vmem] * 6 + [hbm] * 3,
-        out_specs=(hbm, vmem),
+        in_specs=[pl.BlockSpec(memory_space=pltpu.HBM)] * 9,
+        out_specs=(vmem, vmem),
         scratch_shapes=[
             pltpu.VMEM((2, 2, 4, 4, 4, 16, HALF), bf16),
             pltpu.VMEM((features, columns), bf16),
-            pltpu.VMEM((tokens, columns), f32),
+            pltpu.VMEM((2, 4, 4, 4, 16, columns), f32),
             pltpu.VMEM((16, 8, 128), f32),
             pltpu.VMEM((16, 8, 128), f32),
             pltpu.VMEM((16, 8, 128), f32),
             pltpu.VMEM((8, 128), f32),
             pltpu.VMEM((8, 128), f32),
-            dma, dma((PIECES,)),
-            dma((37,)), dma((37,)), dma((19,)), dma((19,)),
+            dma,
+            dma((57,)), dma((57,)), dma((38,)), dma((38,)),
             dma((16,)), dma((16,)), dma((16,)), dma((16,)), dma((16,)), dma((16,)),
             pltpu.VMEM((features, inner), bf16),
             pltpu.VMEM((inner, features), bf16),
             dma((2,)),
+            pltpu.VMEM(hidden.shape, bf16),
+            pltpu.VMEM(routes.shape, jnp.int32),
+            pltpu.VMEM(gates.shape, f32),
+            pltpu.VMEM(gain.shape, f32),
+            pltpu.VMEM(final_gain.shape, f32),
+            pltpu.VMEM(targets.shape, jnp.int32),
+            dma((6,)),
+            pltpu.VMEM((2, 8, features), f32),
+            pltpu.VMEM((8, features + 128), f32),
             pltpu.VMEM((2, 8, features + 128), f32),
             pltpu.VMEM((16, 16, 256), bf16),
             pltpu.VMEM((16, 16, 256), bf16),
@@ -542,46 +619,66 @@
             dma((4,)), dma((4,)), dma((8,)), dma((8,)), dma((16,)), dma((16,)), dma, dma,
         ],
         compiler_params=pltpu.CompilerParams(
-            collective_id=1, has_side_effects=True, vmem_limit_bytes=56 * 1024 * 1024
+            collective_id=1, has_side_effects=True, vmem_limit_bytes=48 * 1024 * 1024
         ),
-    )(hidden, routes, gates, gain, final_gain, targets, weight_in, weight_out, weight)
-
-
-def finish_kernel(logits_ref, norms_ref, lengths_ref, probs_ref, head_ref, loss_ref):
-    step = pl.program_id(0)
+    )(*(pltpu.with_memory_space_constraint(one, pltpu.HBM) for one in operands))
+
+
+def finish_kernel(logits_ref, norms_ref, lengths_ref, probs_hbm, head_hbm, loss_ref, probs, heads, probs_sem, head_sem):
     position = lax.broadcasted_iota(jnp.int32, (1, TGT), 1)
-    for i in range(FINISH):
-        rows = slice(i * TGT, (i + 1) * TGT)
-        shift = jnp.transpose(jnp.broadcast_to(norms_ref[i, 0:1, :], (TGT, TGT)))
-        for tile in range(logits_ref.shape[1] // TGT):
+    groups, columns = logits_ref.shape[0], logits_ref.shape[-1]
+
+    def copies(group):
+        rows = pl.ds(group * TGT, TGT)
+        return (
+            pltpu.make_async_copy(probs.at[rows], probs_hbm.at[rows], probs_sem.at[group]),
+            pltpu.make_async_copy(heads.at[rows], head_hbm.at[rows], head_sem.at[group]),
+        )
+
+    def each(group, _):
+        rows = pl.ds(group * TGT, TGT)
+        shift = jnp.transpose(jnp.broadcast_to(norms_ref[group, 0:1, :], (TGT, TGT)))
+        for tile in range(columns // TGT):
             lanes = slice(tile * TGT, (tile + 1) * TGT)
-            values = logits_ref[rows, lanes]
-            head_ref[rows, lanes] = values.astype(jnp.bfloat16)
-            probs_ref[rows, lanes] = (values - shift).astype(jnp.bfloat16)
-        group = step * FINISH + i
-        loss_ref[pl.ds(group, 1), :] = jnp.where(position < lengths_ref[group], norms_ref[i, 1:2, :], 0.0)
+            values = logits_ref[group, :, :, :, lanes].reshape(TGT, TGT)
+            heads[rows, lanes] = values.astype(jnp.bfloat16)
+            probs[rows, lanes] = (values - shift).astype(jnp.bfloat16)
+        loss_ref[pl.ds(group, 1), :] = jnp.where(position < lengths_ref[group], norms_ref[group, 1:2, :], 0.0)
+        for copy in copies(group):
+            copy.start()
+        return 0
+
+    def done(group, _):
+        for copy in copies(group):
+            copy.wait()
+        return 0
+
+    lax.fori_loop(0, groups, each, 0)
+    lax.fori_loop(0, groups, done, 0)
 
 
 def finish(logits, norms, lengths):
-    tokens, columns = logits.shape
-    groups = tokens // TGT
-    rows = pl.BlockSpec((FINISH * TGT, columns), lambda i: (i, 0))
+    groups, columns = logits.shape[0], logits.shape[-1]
+    tokens = groups * TGT
+    vmem, hbm = pl.BlockSpec(memory_space=pltpu.VMEM), pl.BlockSpec(memory_space=pl.ANY)
     return pl.pallas_call(
         finish_kernel,
         name="finish",
-        grid=(groups // FINISH,),
         out_shape=(
             jax.ShapeDtypeStruct((tokens, columns), jnp.bfloat16),
             jax.ShapeDtypeStruct((tokens, columns), jnp.bfloat16),
             jax.ShapeDtypeStruct((groups, TGT), jnp.float32),
         ),
-        in_specs=[
-            rows,
-            pl.BlockSpec((FINISH, 8, 128), lambda i: (i, 0, 0)),
-            pl.BlockSpec(memory_space=pltpu.SMEM),
+        in_specs=[vmem, vmem, pl.BlockSpec(memory_space=pltpu.SMEM)],
+        out_specs=(hbm, hbm, vmem),
+        scratch_shapes=[
+            pltpu.VMEM((tokens, columns), jnp.bfloat16),
+            pltpu.VMEM((tokens, columns), jnp.bfloat16),
+            pltpu.SemaphoreType.DMA((groups,)),
+            pltpu.SemaphoreType.DMA((groups,)),
         ],
-        out_specs=(rows, rows, pl.BlockSpec((groups, TGT), lambda i: (0, 0))),
-    )(logits, norms, lengths)
+        compiler_params=pltpu.CompilerParams(vmem_limit_bytes=24 * 1024 * 1024),
+    )(pltpu.with_memory_space_constraint(logits, pltpu.VMEM), norms, lengths)
 
 
 def on_device(

time: 130 us -> 124 us (0.954)
  Pallas kernels: 129 us -> 124 us
    pallas_call x2, Pallas kernels: 129 us -> 124 us  [the longest x1 120 us: layer(): pl.pallas_call(layer_kernel, name='layer', out_shape=(pltpu.VMEM((16, 4,...]
where the time goes in v4:
time: 124 us
  Pallas kernels  124 us (100%)
    pallas_call x1, Pallas kernels, layer(): pl.pallas_call(layer_kernel, name='layer', out_shape=(pltpu.VMEM((16, 4,...  120 us
    pallas_call x1, Pallas kernels, finish(): pl.pallas_call(finish_kernel, name='finish', out_shape=(jax.ShapeDtypeStr...  3.79 us

profile of v4, /device:TPU:1, one launch (start us, length us, event | category | flops | bytes accessed | tf_op | source)
XLA Modules:
  0.0 124.3 jit_solution(6862548046114115290)
XLA Ops:
  0.6 0.0 copy-start
  0.6 119.9 %layer.1 = (f32[16,4,4,8,640]{4,3,2,1,0:T(8,128)S(1)}, f32[16,8,128]{2,1,0:T(8,128)S(1)}) custom-call(bf16[8,2048]{1,0:T(8,128)(2,1)} %hidden_hbm.1, s32[2,8]{1,0:T(2,128)} %bitcast.9, f32[2,8]{1,0:T(2,128)} %bitcast.10, f32[1,2048]{1,0:T(1,128)} %bitcast.6, f32[1,2048]{1,0:T(1,128)} %bitcast.7, s32[16,128]{1,0:T(8,128)} %bitcast.8, ...), custom_call_target="tpu_custom_call" | custom-call | tf_op jit(solution)/shard_map/layer/pallas_call | solution.py:572
  120.5 0.0 copy-done
  120.5 3.8 %finish.1 = (bf16[2048,640]{1,0:T(8,128)(2,1)}, bf16[2048,640]{1,0:T(8,128)(2,1)}, f32[16,128]{1,0:T(8,128)}) custom-call(f32[16,4,4,8,640]{4,3,2,1,0:T(8,128)S(1)} %get-tuple-element.8.logits_ref, f32[16,8,128]{2,1,0:T(8,128)S(1)} %get-tuple-element.9.norms_ref, s32[16]{0:T(128)S(1)} %copy-done), custom_call_target="tpu_custom_call" | custom-call | tf_op jit(solution)/shard_map/finish/pallas_call | solution.py:664
Async XLA Ops:
  0.6 119.9 %copy-start = (s32[16]{0:T(128)S(1)}, s32[16]{0:T(128)}, u32[]{:S(2)}) copy-start(s32[16]{0:T(128)} %lengths_ref.1) | copy-start | bytes 196

commit v5 on v4

--- a/solution.py
+++ b/solution.py
@@ -1,3 +1,6 @@
+import functools
+import math
+
 import jax
 import jax.numpy as jnp
 from jax import lax
@@ -137,7 +140,7 @@
         shared.push(lambda core, pos=pos, part=part: block(core, pos, part))
 
 
-def gather(where, g, weight, logits, ring_send, ring_recv, pair_send, pair_recv):
+def gather(where, g, weight, logits, meanwhile, ring_send, ring_recv, pair_send, pair_recv):
     wires, shared = Wires(ring_send, ring_recv), Shared(where, Wires(pair_send, pair_recv))
     x, y, zl, zh = where.x, where.y, where.zl, where.zh
     one, two, three, rest = (0, 256), (256, 384), (640, 384), (256, 768)
@@ -171,9 +174,10 @@
         start, width = lanes
         total = logits[at]
         shape = total.shape
-        total = total.reshape(256, shape[-1])
+        height = math.prod(shape[:-1])
+        total = total.reshape(height, shape[-1])
         for core in (0, 1):
-            rows = g[(core, *at, slice(None), pl.ds(start, width))].reshape(256, width)
+            rows = g[(core, *at, slice(None), pl.ds(start, width))].reshape(height, width)
             columns = weight[core * HALF + start : core * HALF + start + width]
             total = total + jnp.dot(rows, columns, preferred_element_type=jnp.float32)
         logits[at] = total.reshape(shape)
@@ -188,12 +192,11 @@
 
     def over_slabs(count, step):
         def body(i, _):
-            side, ahead = lax.rem(i, 2), step(lax.div(i, 2))
-            multiply((side, slice(None), lax.rem(x + ahead, 4), slice(None)), two)
-            multiply((side, lax.rem(y + ahead, 4), slice(None), slice(None)), three)
+            multiply((slice(None), slice(None), lax.rem(x + step(i), 4), slice(None)), two)
+            multiply((slice(None), lax.rem(y + step(i), 4), slice(None), slice(None)), three)
             return 0
 
-        lax.fori_loop(0, 2 * count, body, 0)
+        lax.fori_loop(0, count, body, 0)
 
     def advance(chains):
         for chain in chains:
@@ -207,6 +210,7 @@
     early, late = [x_last(0), y_last(0)], [x_last(1), y_last(1)]
     advance([by_x, by_z])
     logits[...] = jnp.zeros_like(logits)
+    meanwhile()
     advance([by_x, by_y, by_z] + early + late)
     advance([by_y])
     early, late = [z_last(0)] + early, [z_last(1)] + late
@@ -258,13 +262,15 @@
     return wires, shared.wires
 
 
-def exchange(n, me, to, src, dst, send, recv):
+def exchange(n, me, to, src, dst, send, recv, meanwhile=None):
     def each(i, _):
         other = lax.rem(me + i, n)
         remote(src(other), dst.at[me], send.at[i], recv.at[i], to(other)).start()
         return 0
 
     lax.fori_loop(1, n, each, 0)
+    if meanwhile is not None:
+        meanwhile()
 
     def done(i, _):
         origin = lax.rem(me - i + n, n)
@@ -318,7 +324,7 @@
 
 def experts(
     where, barrier, small, late, hidden_ref, routes_ref, gates_ref, gain_ref, final_gain_ref, weight_in, weight_out, loads, g,
-    local, outbox, pack, outgoing, incoming, rows, units, away, sent_half, near, summed, parts, returning, returned, spread,
+    local, outbox, pack, outgoing, incoming, rows, units, away, sent_half, summed, parts, returning, returned, spread,
     pack_send, pack_recv, go_send, go_recv, row_send, row_recv, rowp_send, rowp_recv, half_send, half_recv,
     sum_send, sum_recv, back_send, back_recv, ln_send, ln_recv,
 ):
@@ -392,10 +398,9 @@
 
     def second(i, _):
         other = lax.rem(where.y + 1 + i, 4)
-        some = units[other]
-        away[other] = jnp.dot(some, weight_out[:, theirs], preferred_element_type=jnp.float32).astype(jnp.bfloat16)
+        found = jnp.dot(units[other], weight_out[:, theirs], preferred_element_type=jnp.float32)
+        away[other] = found.astype(jnp.bfloat16)
         half(i, other).start()
-        near[other] = jnp.dot(some, weight_out[:, mine], preferred_element_type=jnp.float32)
         return 0
 
     lax.fori_loop(0, 4, second, 0)
@@ -405,8 +410,9 @@
 
     def add(i, _):
         other = lax.rem(where.y + 1 + i, 4)
+        near = jnp.dot(units[other], weight_out[:, mine], preferred_element_type=jnp.float32)
         half(i, other).wait_recv()
-        total = (near[other] + sent_half[other].astype(jnp.float32)).astype(jnp.bfloat16)
+        total = (near + sent_half[other].astype(jnp.float32)).astype(jnp.bfloat16)
         summed[pl.ds(other * 2, 2)] = total.reshape(2, 64, HALF)
         for side in (0, 1):
             block = other * 2 + side
@@ -474,8 +480,8 @@
 
 def layer_kernel(
     hidden_hbm, routes_hbm, gates_hbm, gain_hbm, final_gain_hbm, targets_hbm, in_hbm, out_hbm, weight_hbm,
-    kept, norms_ref,
-    g, weight, logits, stats, by_group, by_section, merged, solved,
+    kept, heads, norms_ref,
+    g, weight, logits, wanted, stats, by_group, by_section, merged, solved,
     weight_sem, ring_send, ring_recv, pair_send, pair_recv,
     one_send, one_recv, two_send, two_recv, three_send, three_recv,
     weight_in, weight_out, weight_sems, hidden_ref, routes_ref, gates_ref, gain_ref, final_gain_ref, targets_ref,
@@ -518,7 +524,16 @@
     )
     load.wait()
     small[5].wait()
-    gather(where, g, weight, logits, ring_send, ring_recv, pair_send, pair_recv)
+
+    def spread_targets():
+        def body(group, _):
+            row = targets_ref[pl.ds(group, 1), :].astype(jnp.float32)
+            wanted[group] = jnp.transpose(jnp.broadcast_to(row, (128, 128))).astype(jnp.int32)
+            return 0
+
+        lax.fori_loop(0, 2 * PIECES, body, 0)
+
+    gather(where, g, weight, logits, spread_targets, ring_send, ring_recv, pair_send, pair_recv)
 
     columns = weight.shape[1]
     offset = (where.s * 16 + where.e) * columns
@@ -531,18 +546,17 @@
             part = logits[zl, y, :, :, core * 8 : (core + 1) * 8]
             kept[group] = part
             part = part.reshape(128, columns)
-            top = jnp.max(part, axis=1, keepdims=True)
-            total = jnp.sum(jnp.exp(part - top), axis=1, keepdims=True)
-            wanted = jnp.transpose(
-                jnp.broadcast_to(targets_ref[pl.ds(group, 1), :].astype(jnp.float32), (128, 128))
+            tiles = [part[:, i : i + 128] for i in range(0, columns, 128)]
+            top = functools.reduce(jnp.maximum, tiles)
+            total = sum(jnp.exp(tile - top) for tile in tiles)
+            picked = sum(
+                jnp.where(wanted[group] == lane + (offset + i * 128), tile, 0.0) for i, tile in enumerate(tiles)
             )
-            picked = jnp.zeros((128, 128), jnp.float32)
-            for tile in range(columns // 128):
-                ids = (lane + (offset + tile * 128)).astype(jnp.float32)
-                picked = picked + jnp.where(ids == wanted, part[:, tile * 128 : (tile + 1) * 128], 0.0)
-            picked = jnp.sum(picked, axis=1, keepdims=True)
-            table = jnp.where(lane == 0, top, jnp.where(lane == 1, total, jnp.where(lane == 2, picked, 0.0)))
-            stats[group] = jnp.transpose(table)[0:8]
+            top = jnp.transpose(top)
+            highest = jnp.max(top, axis=0, keepdims=True)
+            total = jnp.sum(jnp.transpose(total) * jnp.exp(top - highest), axis=0, keepdims=True)
+            picked = jnp.sum(jnp.transpose(picked), axis=0, keepdims=True)
+            stats[group] = rows8(highest, total, picked)
         return 0
 
     lax.fori_loop(0, PIECES, chunk, 0)
@@ -550,7 +564,15 @@
     to_expert = lambda other: (where.s, other)
     to_section = lambda other: (other, where.e)
     by_group[where.s] = stats[where.s]
-    exchange(16, where.s, to_section, lambda other: stats.at[other], by_group, one_send, one_recv)
+
+    def round_logits():
+        def body(group, _):
+            heads[pl.ds(group * 128, 128), :] = kept[group].reshape(128, columns).astype(jnp.bfloat16)
+            return 0
+
+        lax.fori_loop(0, 2 * PIECES, body, 0)
+
+    exchange(16, where.s, to_section, lambda other: stats.at[other], by_group, one_send, one_recv, round_logits)
     merged[...] = rows8(*merge(by_group[...]))
     by_section[where.e] = merged[...]
     exchange(16, where.e, to_expert, lambda other: merged, by_section, two_send, two_recv)
@@ -574,14 +596,16 @@
         name="layer",
         out_shape=(
             pltpu.VMEM((16, 4, 4, 8, columns), f32),
-            jax.ShapeDtypeStruct((16, 8, 128), f32),
+            pltpu.VMEM((tokens, columns), bf16),
+            pltpu.VMEM((16, 8, 128), f32),
         ),
         in_specs=[pl.BlockSpec(memory_space=pltpu.HBM)] * 9,
-        out_specs=(vmem, vmem),
+        out_specs=(vmem, vmem, vmem),
         scratch_shapes=[
             pltpu.VMEM((2, 2, 4, 4, 4, 16, HALF), bf16),
             pltpu.VMEM((features, columns), bf16),
             pltpu.VMEM((2, 4, 4, 4, 16, columns), f32),
+            pltpu.VMEM((16, 128, 128), jnp.int32),
             pltpu.VMEM((16, 8, 128), f32),
             pltpu.VMEM((16, 8, 128), f32),
             pltpu.VMEM((16, 8, 128), f32),
@@ -609,7 +633,6 @@
             pltpu.VMEM((4, 128, inner), bf16),
             pltpu.VMEM((4, 128, HALF), bf16),
             pltpu.VMEM((4, 128, HALF), bf16),
-            pltpu.VMEM((4, 128, HALF), f32),
             pltpu.VMEM((8, 64, HALF), bf16),
             pltpu.VMEM((8, 64, HALF), bf16),
             pltpu.VMEM((16, 16, 256), bf16),
@@ -624,16 +647,15 @@
     )(*(pltpu.with_memory_space_constraint(one, pltpu.HBM) for one in operands))
 
 
-def finish_kernel(logits_ref, norms_ref, lengths_ref, probs_hbm, head_hbm, loss_ref, probs, heads, probs_sem, head_sem):
+def finish_kernel(logits_ref, heads_ref, norms_ref, lengths_ref, probs_hbm, head_hbm, loss_ref, probs, probs_sem, head_sem):
     position = lax.broadcasted_iota(jnp.int32, (1, TGT), 1)
     groups, columns = logits_ref.shape[0], logits_ref.shape[-1]
-
-    def copies(group):
+    rounded = pltpu.make_async_copy(heads_ref, head_hbm, head_sem)
+    rounded.start()
+
+    def copy(group):
         rows = pl.ds(group * TGT, TGT)
-        return (
-            pltpu.make_async_copy(probs.at[rows], probs_hbm.at[rows], probs_sem.at[group]),
-            pltpu.make_async_copy(heads.at[rows], head_hbm.at[rows], head_sem.at[group]),
-        )
+        return pltpu.make_async_copy(probs.at[rows], probs_hbm.at[rows], probs_sem.at[group])
 
     def each(group, _):
         rows = pl.ds(group * TGT, TGT)
@@ -641,54 +663,55 @@
         for tile in range(columns // TGT):
             lanes = slice(tile * TGT, (tile + 1) * TGT)
             values = logits_ref[group, :, :, :, lanes].reshape(TGT, TGT)
-            heads[rows, lanes] = values.astype(jnp.bfloat16)
             probs[rows, lanes] = (values - shift).astype(jnp.bfloat16)
+        copy(group).start()
         loss_ref[pl.ds(group, 1), :] = jnp.where(position < lengths_ref[group], norms_ref[group, 1:2, :], 0.0)
-        for copy in copies(group):
-            copy.start()
         return 0
 
     def done(group, _):
-        for copy in copies(group):
-            copy.wait()
+        copy(group).wait()
         return 0
 
     lax.fori_loop(0, groups, each, 0)
     lax.fori_loop(0, groups, done, 0)
-
-
-def finish(logits, norms, lengths):
-    groups, columns = logits.shape[0], logits.shape[-1]
-    tokens = groups * TGT
+    rounded.wait()
+
+
+def finish(logits, heads, norms, lengths):
+    groups = logits.shape[0]
     vmem, hbm = pl.BlockSpec(memory_space=pltpu.VMEM), pl.BlockSpec(memory_space=pl.ANY)
     return pl.pallas_call(
         finish_kernel,
         name="finish",
         out_shape=(
-            jax.ShapeDtypeStruct((tokens, columns), jnp.bfloat16),
-            jax.ShapeDtypeStruct((tokens, columns), jnp.bfloat16),
+            jax.ShapeDtypeStruct(heads.shape, jnp.bfloat16),
+            jax.ShapeDtypeStruct(heads.shape, jnp.bfloat16),
             jax.ShapeDtypeStruct((groups, TGT), jnp.float32),
         ),
-        in_specs=[vmem, vmem, pl.BlockSpec(memory_space=pltpu.SMEM)],
+        in_specs=[vmem, vmem, vmem, pl.BlockSpec(memory_space=pltpu.SMEM)],
         out_specs=(hbm, hbm, vmem),
         scratch_shapes=[
-            pltpu.VMEM((tokens, columns), jnp.bfloat16),
-            pltpu.VMEM((tokens, columns), jnp.bfloat16),
+            pltpu.VMEM(heads.shape, jnp.bfloat16),
             pltpu.SemaphoreType.DMA((groups,)),
-            pltpu.SemaphoreType.DMA((groups,)),
+            pltpu.SemaphoreType.DMA,
         ],
         compiler_params=pltpu.CompilerParams(vmem_limit_bytes=24 * 1024 * 1024),
-    )(pltpu.with_memory_space_constraint(logits, pltpu.VMEM), norms, lengths)
+    )(
+        pltpu.with_memory_space_constraint(logits, pltpu.VMEM),
+        pltpu.with_memory_space_constraint(heads, pltpu.VMEM),
+        pltpu.with_memory_space_constraint(norms, pltpu.VMEM),
+        lengths,
+    )
 
 
 def on_device(
     hidden, routes, gates, targets, target_lengths, moe_gain, fc_in, fc_out, final_gain, head_weight
 ):
     wanted = targets.reshape(-1, TGT)
-    logits, norms = layer(
+    logits, heads, norms = layer(
         hidden, routes.T, gates.T, moe_gain[None], final_gain[None], wanted, fc_in, fc_out, head_weight
     )
-    log_probs, head_logits, loss = finish(logits, norms, target_lengths)
+    log_probs, head_logits, loss = finish(logits, heads, norms, target_lengths)
     return (log_probs, head_logits, loss.reshape(-1))
 
 

time: 124 us -> 122 us (0.984)
  Pallas kernels: 124 us -> 122 us
    pallas_call x1, Pallas kernels: 120 us -> 118 us  [layer(): pl.pallas_call(layer_kernel, name='layer', out_shape=(pltpu.VMEM((16, 4,...]
where the time goes in v5:
time: 122 us
  Pallas kernels  122 us (100%)
    pallas_call x1, Pallas kernels, layer(): pl.pallas_call(layer_kernel, name='layer', out_shape=(pltpu.VMEM((16, 4,...  118 us
    pallas_call x1, Pallas kernels, finish(): pl.pallas_call(finish_kernel, name='finish', out_shape=(jax.ShapeDtypeStr...  3.62 us

profile of v5, /device:TPU:1, one launch (start us, length us, event | category | flops | bytes accessed | tf_op | source)
XLA Modules:
  0.0 122.3 jit_solution(12849125410384115954)
XLA Ops:
  0.6 0.0 copy-start
  0.6 118.0 %layer.1 = (f32[16,4,4,8,640]{4,3,2,1,0:T(8,128)S(1)}, bf16[2048,640]{1,0:T(8,128)(2,1)S(1)}, f32[16,8,128]{2,1,0:T(8,128)S(1)}) custom-call(bf16[8,2048]{1,0:T(8,128)(2,1)} %hidden_hbm.1, s32[2,8]{1,0:T(2,128)} %bitcast.9, f32[2,8]{1,0:T(2,128)} %bitcast.10, f32[1,2048]{1,0:T(1,128)} %bitcast.6, f32[1,2048]{1,0:T(1,128)} %bitcast.7, s32[16,128]{1,0:T(8,128)} %bitcast.8, ...), custom_call_target="tpu_custom_call" | custom-call | tf_op jit(solution)/shard_map/layer/pallas_call | solution.py:594
  118.6 0.0 copy-done
  118.6 3.6 %finish.1 = (bf16[2048,640]{1,0:T(8,128)(2,1)}, bf16[2048,640]{1,0:T(8,128)(2,1)}, f32[16,128]{1,0:T(8,128)}) custom-call(f32[16,4,4,8,640]{4,3,2,1,0:T(8,128)S(1)} %get-tuple-element.9.logits_ref, bf16[2048,640]{1,0:T(8,128)(2,1)S(1)} %get-tuple-element.10.heads_ref, f32[16,8,128]{2,1,0:T(8,128)S(1)} %get-tuple-element.11.norms_ref, s32[16]{0:T(128)S(1)} %copy-done), custom_call_target="tpu_custom_call" | custom-call | tf_op jit(solution)/shard_map/finish/pallas_call | solution.py:683
Async XLA Ops:
  0.6 118.0 %copy-start = (s32[16]{0:T(128)S(1)}, s32[16]{0:T(128)}, u32[]{:S(2)}) copy-start(s32[16]{0:T(128)} %lengths_ref.1) | copy-start | bytes 196

commit v6 on v5

--- a/solution.py
+++ b/solution.py
@@ -83,9 +83,10 @@
 def straight(where, wires, axis, n, block):
     me = where.at(axis)
     mine = block(where.core, me)
-    numbers = [wires.push(mine, mine, where.beside(axis, i)) for i in range(1, n)]
+    order = sorted(range(1, n), key=lambda i: -min(i, n - i))
+    numbers = [wires.push(mine, mine, where.beside(axis, i)) for i in order]
     yield
-    for i, k in enumerate(numbers, 1):
+    for i, k in zip(order, numbers):
         wires.pull(k, block(where.core, lax.rem(me - i + n, n)), where.beside(axis, -i))
 
 
@@ -120,7 +121,7 @@
     me = where.z
     numbers = []
     mine = block(where.core, me)
-    for step in (1, -1, 2, -2):
+    for step in (2, -2, 1, -1):
         numbers.append((wires.push(mine, mine, where.beside("z", step)), step))
     yield
     for k, step in numbers:
@@ -130,7 +131,7 @@
     numbers = []
     for side, sign in ((0, 1), (1, -1)):
         pos = lax.rem(me - 2 * sign + 8, 8)
-        for step, part in ((sign, None), (2 * sign, side)):
+        for step, part in ((2 * sign, side), (sign, None)):
             mine = block(where.core, pos, part)
             numbers.append((wires.push(mine, mine, where.beside("z", step)), step, sign, part))
     yield
@@ -170,30 +171,29 @@
         shared.push(lambda core: block(core, y))
         yield from ring(where, wires, "y", 4, block, shared)
 
-    def multiply(at, lanes):
+    def multiply(core, at, lanes):
         start, width = lanes
         total = logits[at]
         shape = total.shape
         height = math.prod(shape[:-1])
         total = total.reshape(height, shape[-1])
-        for core in (0, 1):
-            rows = g[(core, *at, slice(None), pl.ds(start, width))].reshape(height, width)
-            columns = weight[core * HALF + start : core * HALF + start + width]
-            total = total + jnp.dot(rows, columns, preferred_element_type=jnp.float32)
+        rows = g[(core, *at, slice(None), pl.ds(start, width))].reshape(height, width)
+        columns = weight[pl.ds(pl.multiple_of(core * HALF + start, 128), width), :]
+        total = total + jnp.dot(rows, columns, preferred_element_type=jnp.float32)
         logits[at] = total.reshape(shape)
 
-    def over_planes(count, step):
+    def over_planes(core, count, step):
         def body(i, _):
             pos = lax.rem(where.z + step(i), 8)
-            multiply((lax.rem(pos, 2), slice(None), slice(None), lax.div(pos, 2)), one)
+            multiply(core, (lax.rem(pos, 2), slice(None), slice(None), lax.div(pos, 2)), one)
             return 0
 
         lax.fori_loop(0, count, body, 0)
 
-    def over_slabs(count, step):
+    def over_slabs(core, count, step):
         def body(i, _):
-            multiply((slice(None), slice(None), lax.rem(x + step(i), 4), slice(None)), two)
-            multiply((slice(None), lax.rem(y + step(i), 4), slice(None), slice(None)), three)
+            multiply(core, (slice(None), slice(None), lax.rem(x + step(i), 4), slice(None)), two)
+            multiply(core, (slice(None), lax.rem(y + step(i), 4), slice(None), slice(None)), three)
             return 0
 
         lax.fori_loop(0, count, body, 0)
@@ -214,18 +214,18 @@
     advance([by_x, by_y, by_z] + early + late)
     advance([by_y])
     early, late = [z_last(0)] + early, [z_last(1)] + late
-    advance(early + late)
-    shared.pull()
-    over_planes(1, lambda i: 0)
-    over_slabs(1, lambda i: 0)
-    advance(early + late)
-    shared.pull()
-    over_planes(4, lambda i: i + 1 + 3 * lax.div(i, 2))
-    over_slabs(2, lambda i: 2 * i + 1)
-    advance(early + late)
-    shared.pull()
-    over_planes(3, lambda i: i + 3)
-    over_slabs(1, lambda i: 2)
+    rounds = (
+        (1, lambda i: 0, 1, lambda i: 0),
+        (4, lambda i: i + 1 + 3 * lax.div(i, 2), 2, lambda i: 2 * i + 1),
+        (3, lambda i: i + 3, 1, lambda i: 2),
+    )
+    for planes_in, plane_step, slabs_in, slab_step in rounds:
+        advance(early + late)
+        for core in (where.core, 1 - where.core):
+            if core is not where.core:
+                shared.pull()
+            over_planes(core, planes_in, plane_step)
+            over_slabs(core, slabs_in, slab_step)
     wires.drain()
     shared.wires.drain()
 

time: 122 us -> 120 us (0.984)
  Pallas kernels: 122 us -> 119 us
    pallas_call x1, Pallas kernels: 118 us -> 115 us  [layer(): pl.pallas_call(layer_kernel, name='layer', out_shape=(pltpu.VMEM((16, 4,...]
where the time goes in v6:
time: 120 us; the launch traced here: 119 us
  Pallas kernels  119 us (99%)
    pallas_call x1, Pallas kernels, layer(): pl.pallas_call(layer_kernel, name='layer', out_shape=(pltpu.VMEM((16, 4,...  115 us
    pallas_call x1, Pallas kernels, finish(): pl.pallas_call(finish_kernel, name='finish', out_shape=(jax.ShapeDtypeStr...  3.62 us

profile of v6, /device:TPU:1, one launch (start us, length us, event | category | flops | bytes accessed | tf_op | source)
XLA Modules:
  0.0 119.5 jit_solution(14600225172613279747)
XLA Ops:
  0.6 0.0 copy-start
  0.6 115.2 %layer.1 = (f32[16,4,4,8,640]{4,3,2,1,0:T(8,128)S(1)}, bf16[2048,640]{1,0:T(8,128)(2,1)S(1)}, f32[16,8,128]{2,1,0:T(8,128)S(1)}) custom-call(bf16[8,2048]{1,0:T(8,128)(2,1)} %hidden_hbm.1, s32[2,8]{1,0:T(2,128)} %bitcast.9, f32[2,8]{1,0:T(2,128)} %bitcast.10, f32[1,2048]{1,0:T(1,128)} %bitcast.6, f32[1,2048]{1,0:T(1,128)} %bitcast.7, s32[16,128]{1,0:T(8,128)} %bitcast.8, ...), custom_call_target="tpu_custom_call" | custom-call | tf_op jit(solution)/shard_map/layer/pallas_call | solution.py:594
  115.9 0.0 copy-done
  115.9 3.6 %finish.1 = (bf16[2048,640]{1,0:T(8,128)(2,1)}, bf16[2048,640]{1,0:T(8,128)(2,1)}, f32[16,128]{1,0:T(8,128)}) custom-call(f32[16,4,4,8,640]{4,3,2,1,0:T(8,128)S(1)} %get-tuple-element.9.logits_ref, bf16[2048,640]{1,0:T(8,128)(2,1)S(1)} %get-tuple-element.10.heads_ref, f32[16,8,128]{2,1,0:T(8,128)S(1)} %get-tuple-element.11.norms_ref, s32[16]{0:T(128)S(1)} %copy-done), custom_call_target="tpu_custom_call" | custom-call | tf_op jit(solution)/shard_map/finish/pallas_call | solution.py:683
Async XLA Ops:
  0.6 115.2 %copy-start = (s32[16]{0:T(128)S(1)}, s32[16]{0:T(128)}, u32[]{:S(2)}) copy-start(s32[16]{0:T(128)} %lengths_ref.1) | copy-start | bytes 196

commit v7 on v6

--- a/solution.py
+++ b/solution.py
@@ -258,8 +258,7 @@
         yield from ring(where, wires, "y", 4, block, shared)
 
     together(z_last(), y_last())
-    shared.pull()
-    return wires, shared.wires
+    return wires, shared
 
 
 def exchange(n, me, to, src, dst, send, recv, meanwhile=None):
@@ -324,7 +323,7 @@
 
 def experts(
     where, barrier, small, late, hidden_ref, routes_ref, gates_ref, gain_ref, final_gain_ref, weight_in, weight_out, loads, g,
-    local, outbox, pack, outgoing, incoming, rows, units, away, sent_half, summed, parts, returning, returned, spread,
+    local, outbox, begun, pack, outgoing, incoming, rows, units, away, sent_half, summed, parts, returning, returned, spread,
     pack_send, pack_recv, go_send, go_recv, row_send, row_recv, rowp_send, rowp_recv, half_send, half_recv,
     sum_send, sum_recv, back_send, back_recv, ln_send, ln_recv,
 ):
@@ -379,19 +378,27 @@
     for j in range(QUARTERS):
         rows[core, where.y, where.zl, :, j * 256 : (j + 1) * 256] = arrived[j * 64 : (j + 1) * 64].astype(jnp.bfloat16)
 
-    wires, pairs = spread_rows(where, rows, row_send, row_recv, rowp_send, rowp_recv)
+    wires, shared = spread_rows(where, rows, row_send, row_recv, rowp_send, rowp_recv)
     loads[0].wait()
     loads[1].wait()
 
-    def first(i, _):
-        low = rows[0, pl.ds(i * 2, 2)].reshape(256, HALF)
-        high = rows[1, pl.ds(i * 2, 2)].reshape(256, HALF)
-        found = jnp.dot(low, weight_in[0:HALF], preferred_element_type=jnp.float32)
-        found = found + jnp.dot(high, weight_in[HALF:], preferred_element_type=jnp.float32)
+    def first(half_of, i):
+        some_rows = rows[half_of, pl.ds(i * 2, 2)].reshape(256, HALF)
+        some_weights = weight_in[pl.ds(pl.multiple_of(half_of * HALF, HALF), HALF), :]
+        return jnp.dot(some_rows, some_weights, preferred_element_type=jnp.float32)
+
+    def first_own(i, _):
+        begun[i] = first(core, i)
+        return 0
+
+    def first_other(i, _):
+        found = begun[i] + first(1 - core, i)
         units[pl.ds(i * 2, 2)] = jnp.maximum(found, 0.0).astype(jnp.bfloat16).reshape(2, 128, -1)
         return 0
 
-    lax.fori_loop(0, 2, first, 0)
+    lax.fori_loop(0, 2, first_own, 0)
+    shared.pull()
+    lax.fori_loop(0, 2, first_other, 0)
 
     def half(i, other):
         return remote(away.at[other], sent_half.at[other], half_send.at[i], half_recv.at[i], where.sibling)
@@ -463,7 +470,7 @@
     g[core, where.zl, where.y, where.x, where.zh] = final.astype(jnp.bfloat16)
 
     wires.drain()
-    pairs.drain()
+    shared.wires.drain()
 
     def halves_left(i, _):
         half(i, lax.rem(where.y + 1 + i, 4)).wait_send()
@@ -626,6 +633,7 @@
             dma((6,)),
             pltpu.VMEM((2, 8, features), f32),
             pltpu.VMEM((8, features + 128), f32),
+            pltpu.VMEM((2, 256, inner), f32),
             pltpu.VMEM((2, 8, features + 128), f32),
             pltpu.VMEM((16, 16, 256), bf16),
             pltpu.VMEM((16, 16, 256), bf16),

time: 120 us -> 119 us (level)
  no operation moved by 1% of the time
where the time goes in v7:
time: 119 us
  Pallas kernels  118 us (99%)
    pallas_call x1, Pallas kernels, layer(): pl.pallas_call(layer_kernel, name='layer', out_shape=(pltpu.VMEM((16, 4,...  115 us
    pallas_call x1, Pallas kernels, finish(): pl.pallas_call(finish_kernel, name='finish', out_shape=(jax.ShapeDtypeStr...  3.62 us

profile of v7, /device:TPU:1, one launch (start us, length us, event | category | flops | bytes accessed | tf_op | source)
XLA Modules:
  0.0 119.2 jit_solution(3065621556059735210)
XLA Ops:
  0.6 0.0 copy-start
  0.6 114.9 %layer.1 = (f32[16,4,4,8,640]{4,3,2,1,0:T(8,128)S(1)}, bf16[2048,640]{1,0:T(8,128)(2,1)S(1)}, f32[16,8,128]{2,1,0:T(8,128)S(1)}) custom-call(bf16[8,2048]{1,0:T(8,128)(2,1)} %hidden_hbm.1, s32[2,8]{1,0:T(2,128)} %bitcast.9, f32[2,8]{1,0:T(2,128)} %bitcast.10, f32[1,2048]{1,0:T(1,128)} %bitcast.6, f32[1,2048]{1,0:T(1,128)} %bitcast.7, s32[16,128]{1,0:T(8,128)} %bitcast.8, ...), custom_call_target="tpu_custom_call" | custom-call | tf_op jit(solution)/shard_map/layer/pallas_call | solution.py:601
  115.5 0.0 copy-done
  115.5 3.6 %finish.1 = (bf16[2048,640]{1,0:T(8,128)(2,1)}, bf16[2048,640]{1,0:T(8,128)(2,1)}, f32[16,128]{1,0:T(8,128)}) custom-call(f32[16,4,4,8,640]{4,3,2,1,0:T(8,128)S(1)} %get-tuple-element.9.logits_ref, bf16[2048,640]{1,0:T(8,128)(2,1)S(1)} %get-tuple-element.10.heads_ref, f32[16,8,128]{2,1,0:T(8,128)S(1)} %get-tuple-element.11.norms_ref, s32[16]{0:T(128)S(1)} %copy-done), custom_call_target="tpu_custom_call" | custom-call | tf_op jit(solution)/shard_map/finish/pallas_call | solution.py:691
Async XLA Ops:
  0.6 114.9 %copy-start = (s32[16]{0:T(128)S(1)}, s32[16]{0:T(128)}, u32[]{:S(2)}) copy-start(s32[16]{0:T(128)} %lengths_ref.1) | copy-start | bytes 196
